TPU v7x, 512 devices: a whole 4x4x16 slice. The times are simulated.
512 devices in a mesh: seq: 64 (over z_lo, x, core), head: 8 (over y, z_hi).
Axes of the slice: x: 4, y: 4, z: 16 (z_hi: 2, z_lo: 8; z = z_hi * 8 + z_lo), core: 2. Of those that a mesh axis runs over, the one named last changes fastest.
Arguments:
- layer_input: bfloat16 [8192, 8192], P('seq', 'head'), may hold values from -6 to 6
- queries: bfloat16 [8192, 4096], P('seq', 'head'), may hold values from -32 to 32
- key_states: bfloat16 [8192, 1024], P('seq', 'head'), may hold values from -32 to 32
- value_states: bfloat16 [8192, 1024], P('seq', 'head'), may hold values from -6 to 6
- out_grad: bfloat16 [8192, 4096], P('seq', 'head'), may hold values from -24 to 24
- input_hash: int32 [2, 8192], P(None, 'head'), may hold values from 0 to 63
- query_hash: int32 [2, 4096], P(None, 'head'), may hold values from 0 to 63
- key_hash: int32 [2, 1024], P(None, 'head'), may hold values from 0 to 63
- value_hash: int32 [2, 1024], P(None, 'head'), may hold values from 0 to 63
- doc_starts: int32 [64], replicated, may hold values from 0 to 8128, as said below
- doc_rows: int32 [64], replicated, may hold values from 0 to 63, each once
Outputs:
- sketches: float32 [64, 3, 4096], P('seq', None, 'head')
Inputs may be any that keep to these rules, and one draw needn't show every extreme that they name: `input_hash`: row 0 holds each input feature's bucket; row 1 its sign: +1 where even, -1 where odd. `query_hash`: row 0 holds each query feature's bucket; row 1 its sign: +1 where even, -1 where odd. `key_hash`: row 0 holds each key feature's bucket; row 1 its sign: +1 where even, -1 where odd. `value_hash`: row 0 holds each value feature's bucket; row 1 its sign: +1 where even, -1 where odd. `doc_starts`: increasing; the first is 0; a document starts at every multiple of 512; every document holds 64 to 320 tokens, both reached, so the 128 tokens of one device touch at most 3 documents, and some device's touch 3. `doc_rows`: each output row receives exactly one document.
All inputs are finite; a program needn't handle non-finite values.
Results may differ from a plain program's by a relative error of at most 0.015.
Values may be sent and summed in bfloat16 or wider, within the bound.
A program may use at most 64 MiB of HBM per device.

v0:
```python
import math

import jax
import jax.numpy as jnp
from jax import lax
from jax.sharding import PartitionSpec as P

D = 8192
SK = 64


masked_score = -1e30
highest = lax.Precision.HIGHEST


def from_behind(value, axis, steps):
    count = lax.axis_size(axis)
    pairs = [(source, (source + steps) % count) for source in range(count)]
    return lax.ppermute(value, axis, pairs)


def from_behind_2(value, axis, steps):
    count = lax.axis_size(axis)
    initial, last = (max(0, -steps), min(count, count - steps))
    return lax.ppermute(value, axis, [(source, source + steps) for source in range(initial, last)])


def signed_table(hashes, buckets_count):
    matches = hashes[0][:, None] == jnp.arange(buckets_count, dtype=jnp.int32)[None, :]
    sign_values = 1 - 2 * (hashes[1] % 2)
    return jnp.where(matches, sign_values[:, None], 0).astype(jnp.bfloat16)


def sketch_part(rows_in, hashes, full_width):
    sign_table = signed_table(hashes, SK)
    return jnp.dot(rows_in, sign_table, preferred_element_type=jnp.float32) * math.sqrt(
        SK / full_width
    )


def on_device(
    layer_input,
    queries,
    key_states,
    value_states,
    out_grad,
    input_hash,
    query_hash,
    key_hash,
    value_hash,
    doc_starts,
    doc_rows,
):
    token_rows, per_head_width = key_states.shape
    query_heads = queries.shape[1] // per_head_width
    seq_count = lax.axis_size("seq")
    head_count = lax.axis_size("head")
    seq_place = lax.axis_index("seq")
    score_scale = 1.0 / math.sqrt(per_head_width)
    key_span = 4 * token_rows
    head_row_entries = token_rows * query_heads
    query_rows = queries.reshape(head_row_entries, per_head_width)
    grad_rows = out_grad.reshape(head_row_entries, per_head_width)
    query_places = (
        seq_place * token_rows + jnp.arange(head_row_entries, dtype=jnp.int32) // query_heads
    )
    last_query = seq_place * token_rows + token_rows - 1
    input_part = sketch_part(layer_input, input_hash, D)
    every_key_row, every_value_row = (
        lax.all_gather(key_states, "seq", axis=0, tiled=True),
        lax.all_gather(value_states, "seq", axis=0, tiled=True),
    )
    block_count = every_key_row.shape[0] // key_span

    def masked_scores(key_block, key_places):
        causal = key_places[None, :] <= query_places[:, None]
        scores = (
            jnp.einsum("rd,kd->rk", query_rows, key_block, preferred_element_type=jnp.float32)
            * score_scale
        )
        return (causal, scores)

    def stats_step(block_index, iteration_state):
        first_key = block_index * key_span

        def stats_visit_block(running):
            row_top, row_total = running
            key_block = lax.dynamic_slice_in_dim(every_key_row, first_key, key_span, 0)
            causal, scores = masked_scores(
                key_block, first_key + jnp.arange(key_span, dtype=jnp.int32)
            )
            scores = jnp.where(causal, scores, masked_score)
            new_top = jnp.maximum(row_top, jnp.max(scores, axis=1))
            row_total = row_total * jnp.exp(row_top - new_top) + jnp.sum(
                jnp.exp(scores - new_top[:, None]), axis=1
            )
            return (new_top, row_total)

        return lax.cond(
            first_key <= last_query, stats_visit_block, lambda unchanged: unchanged, iteration_state
        )

    start_top = jnp.full((head_row_entries,), masked_score, jnp.float32)
    row_top, row_total = lax.fori_loop(
        0, block_count, stats_step, (start_top, jnp.zeros((head_row_entries,), jnp.float32))
    )
    log_total = row_top + jnp.log(row_total)

    def probabilities(key_block, key_places):
        causal, scores = masked_scores(key_block, key_places)
        return jnp.where(causal, jnp.exp(scores - log_total[:, None]), 0.0)

    def output_step(block_index, attended):
        first_key = block_index * key_span

        def output_visit_block(running):
            key_block = lax.dynamic_slice_in_dim(every_key_row, first_key, key_span, 0)
            value_block = lax.dynamic_slice_in_dim(every_value_row, first_key, key_span, 0)
            weights = probabilities(key_block, first_key + jnp.arange(key_span, dtype=jnp.int32))
            return running + jnp.dot(
                weights.astype(jnp.bfloat16), value_block, preferred_element_type=jnp.float32
            )

        return lax.cond(
            first_key <= last_query, output_visit_block, lambda unchanged: unchanged, attended
        )

    attended = lax.fori_loop(
        0, block_count, output_step, jnp.zeros((head_row_entries, per_head_width), jnp.float32)
    )
    row_delta = jnp.sum(grad_rows.astype(jnp.float32) * attended, axis=1)
    offsets = (0, 1, 2, 3)
    strides = (4, 4, 4, 4)
    offset_table = jnp.array(offsets, jnp.int32)
    stride_table = jnp.array(strides, jnp.int32)
    row_steps = jnp.arange(token_rows, dtype=jnp.int32)

    def backward_step(step_index, iteration_state):
        couriers, query_accumulator = iteration_state
        blocks = jnp.mod(seq_place - offset_table - stride_table * step_index, seq_count)
        block_beginnings = blocks * token_rows
        key_block = jnp.concatenate(
            [
                lax.dynamic_slice_in_dim(
                    every_key_row, block_beginnings[courier_position], token_rows, 0
                )
                for courier_position in range(4)
            ],
            axis=0,
        )
        value_block = jnp.concatenate(
            [
                lax.dynamic_slice_in_dim(
                    every_value_row, block_beginnings[courier_position], token_rows, 0
                )
                for courier_position in range(4)
            ],
            axis=0,
        )
        key_places = (block_beginnings[:, None] + row_steps[None, :]).reshape(-1)

        def backward_visit_block(running):
            held_grads, query_sum = running
            weights = probabilities(key_block, key_places)
            weights_low = weights.astype(jnp.bfloat16)
            weight_grads = jnp.einsum(
                "rd,kd->rk", grad_rows, value_block, preferred_element_type=jnp.float32
            )
            score_grads = (weights * (weight_grads - row_delta[:, None])).astype(jnp.bfloat16)
            query_sum = query_sum + jnp.dot(
                score_grads, key_block, preferred_element_type=jnp.float32
            )
            key_terms = jnp.einsum(
                "rk,rd->kd", score_grads, query_rows, preferred_element_type=jnp.float32
            )
            value_terms = jnp.einsum(
                "rk,rd->kd", weights_low, grad_rows, preferred_element_type=jnp.float32
            )
            update = jnp.concatenate([key_terms, value_terms], axis=1).reshape(
                4, token_rows, 2 * per_head_width
            )
            return (held_grads + update, query_sum)

        couriers, query_accumulator = lax.cond(
            jnp.min(block_beginnings) <= last_query,
            backward_visit_block,
            lambda unchanged: unchanged,
            (couriers, query_accumulator),
        )
        couriers = from_behind(couriers, "seq", 4)
        return (couriers, query_accumulator)

    initial_couriers = jnp.zeros((4, token_rows, 2 * per_head_width), jnp.float32)
    couriers, query_accumulator = lax.fori_loop(
        0,
        seq_count // 4,
        backward_step,
        (initial_couriers, jnp.zeros((head_row_entries, per_head_width), jnp.float32)),
    )
    resident_gradients = couriers[3]
    for courier_position in (2, 1, 0):
        resident_gradients = (
            from_behind_2(resident_gradients, "seq", -1) + couriers[courier_position]
        )
    key_grads = (resident_gradients[:, :per_head_width] * score_scale).astype(jnp.bfloat16)
    value_grads = resident_gradients[:, per_head_width:].astype(jnp.bfloat16)
    query_grads = (
        (query_accumulator * score_scale)
        .astype(jnp.bfloat16)
        .reshape(token_rows, query_heads * per_head_width)
    )
    grad_parts = jnp.concatenate(
        [
            sketch_part(query_grads, query_hash, queries.shape[1] * head_count),
            sketch_part(key_grads, key_hash, per_head_width * head_count),
            sketch_part(value_grads, value_hash, per_head_width * head_count),
        ],
        axis=1,
    )
    summed = lax.psum(
        jnp.concatenate([input_part, grad_parts], axis=1).reshape(-1), "head"
    ).reshape(token_rows, 4 * SK)
    input_sketch = summed[:, :SK]
    grad_sketch = summed[:, SK:]
    band_rows = SK // head_count
    input_band = lax.dynamic_slice_in_dim(
        input_sketch, lax.axis_index("head") * band_rows, band_rows, 1
    )
    products = (input_band[:, None, :, None] * grad_sketch.reshape(token_rows, 3, 1, SK)).reshape(
        token_rows, 3 * band_rows * SK
    )
    token_places = seq_place * token_rows + jnp.arange(token_rows, dtype=jnp.int32)
    doc_of = jnp.sum((doc_starts[None, :] <= token_places[:, None]).astype(jnp.int32), axis=1) - 1
    slot_hot = ((doc_of - doc_of[0])[:, None] == jnp.arange(3, dtype=jnp.int32)[None, :]).astype(
        jnp.float32
    )
    partials = jnp.einsum(
        "ts,tc->sc", slot_hot, products, precision=highest, preferred_element_type=jnp.float32
    )
    everyone = lax.all_gather(partials, "seq", axis=0, tiled=True)
    block_firsts = jnp.arange(seq_count, dtype=jnp.int32) * token_rows
    first_docs = (
        jnp.sum((doc_starts[None, :] <= block_firsts[:, None]).astype(jnp.int32), axis=1) - 1
    )
    last_docs = (
        jnp.sum(
            (doc_starts[None, :] <= block_firsts[:, None] + token_rows - 1).astype(jnp.int32),
            axis=1,
        )
        - 1
    )
    slot_docs = first_docs[:, None] + jnp.arange(3, dtype=jnp.int32)[None, :]
    slot_live = (slot_docs <= last_docs[:, None]).reshape(-1)
    doc_count = doc_starts.shape[0]
    doc_match = slot_docs.reshape(-1)[:, None] == jnp.arange(doc_count, dtype=jnp.int32)[None, :]
    slot_targets = jnp.sum(jnp.where(doc_match, doc_rows[None, :], 0), axis=1)
    owned_rows = doc_count // seq_count
    my_rows = seq_place * owned_rows + jnp.arange(owned_rows, dtype=jnp.int32)
    row_picks = (slot_live[:, None] & (slot_targets[:, None] == my_rows[None, :])).astype(
        jnp.float32
    )
    gathered_sums = jnp.einsum(
        "mo,mc->oc", row_picks, everyone, precision=highest, preferred_element_type=jnp.float32
    )
    return gathered_sums.reshape(owned_rows, 3, band_rows * SK)


def solution(mesh):
    return jax.shard_map(
        on_device,
        mesh=mesh,
        in_specs=(
            P("seq", "head"),
            P("seq", "head"),
            P("seq", "head"),
            P("seq", "head"),
            P("seq", "head"),
            P(None, "head"),
            P(None, "head"),
            P(None, "head"),
            P(None, "head"),
            P(),
            P(),
        ),
        out_specs=P("seq", None, "head"),
        check_vma=False,
    )
```

profile of v0, /device:TPU:1, one launch (start us, length us, event | category | flops | bytes accessed | tf_op | source)
XLA Modules:
  0.0 1078.5 jit_solution(10510826060525411062)
XLA Ops:
  8.1 1.0 reshape.263
  9.1 1.0 reshape.264
  15.7 120.2 %all-gather.5.cloned.1.call-done = bf16[8192,128]{1,0:T(8,128)(2,1)} async-done(((bf16[128,128]{1,0:T(8,128)(2,1)}), bf16[8192,128]{1,0:T(8,128)(2,1)}) %all-gather.5.cloned.1.call-update) | async-done | bytes 2097168 | tf_op jit(solution)/shard_map/all_gather | solution.py:70
  135.9 2.5 while.52
  135.9 1.5 conditional.11
  136.0 1.2 fusion.94
  138.4 116.1 %all-gather.7.cloned.1.call-done = bf16[8192,128]{1,0:T(8,128)(2,1)} async-done(((bf16[128,128]{1,0:T(8,128)(2,1)}), bf16[8192,128]{1,0:T(8,128)(2,1)}) %all-gather.7.cloned.1.call-update) | async-done | bytes 2097168 | tf_op jit(solution)/shard_map/all_gather | solution.py:71
  254.5 2.7 while.53
  254.6 1.7 conditional.12
  254.6 1.7 fusion.22
  257.5 518.0 %while.54 = (s32[]{:T(128)}, f32[4,128,256]{1,0,2:T(4,128)S(1)}, f32[512,128]{1,0:T(8,128)S(1)}, s32[]{:T(128)}, s32[]{:T(128)}, /*index=5*/bf16[8192,128]{1,0:T...) while((s32[]{:T(128)}, f32[4,128,256]{1,0,2:T(4,128)S(1)}, ...), condition=%wide.region_19.20_spmd.clone.clone, body=%wide.region_15.19_spmd.sunk.clone.clone.sunk | while | flops 339022976 | bytes 14575315 | solution.py:194
  268.3 2.1 conditional.13
  270.4 4.5 collective-permute-start
  274.9 40.0 %collective-permute-done = f32[4,128,256]{1,0,2:T(4,128)S(1)} collective-permute-done((f32[4,128,256]{1,0,2:T(4,128)S(1)}, f32[4,128,256]{1,0,2:T(4,128)S(1)}, u32[]{:S(2)}, u32[]{:S(2)}) %collective-permute-start) | collective-permute-done | bytes 524320 | tf_op jit(solution)/shard_map/while/body/eval_jaxpr/ppermute | solution.py:19
  324.6 1.0 constant_dynamic-slice_fusion.10
  325.7 1.9 collective-permute-start
  327.6 21.6 %collective-permute-done = f32[4,128,256]{1,0,2:T(4,128)S(1)} collective-permute-done((f32[4,128,256]{1,0,2:T(4,128)S(1)}, f32[4,128,256]{1,0,2:T(4,128)S(1)}, u32[]{:S(2)}, u32[]{:S(2)}) %collective-permute-start) | collective-permute-done | bytes 524320 | tf_op jit(solution)/shard_map/while/body/eval_jaxpr/ppermute | solution.py:19
  359.1 1.0 constant_dynamic-slice_fusion.10
  360.1 1.9 collective-permute-start
  362.1 20.7 %collective-permute-done = f32[4,128,256]{1,0,2:T(4,128)S(1)} collective-permute-done((f32[4,128,256]{1,0,2:T(4,128)S(1)}, f32[4,128,256]{1,0,2:T(4,128)S(1)}, u32[]{:S(2)}, u32[]{:S(2)}) %collective-permute-start) | collective-permute-done | bytes 524320 | tf_op jit(solution)/shard_map/while/body/eval_jaxpr/ppermute | solution.py:19
  392.6 1.0 constant_dynamic-slice_fusion.10
  393.6 1.9 collective-permute-start
  395.6 19.8 %collective-permute-done = f32[4,128,256]{1,0,2:T(4,128)S(1)} collective-permute-done((f32[4,128,256]{1,0,2:T(4,128)S(1)}, f32[4,128,256]{1,0,2:T(4,128)S(1)}, u32[]{:S(2)}, u32[]{:S(2)}) %collective-permute-start) | collective-permute-done | bytes 524320 | tf_op jit(solution)/shard_map/while/body/eval_jaxpr/ppermute | solution.py:19
  426.2 1.9 collective-permute-start
  428.1 18.9 %collective-permute-done = f32[4,128,256]{1,0,2:T(4,128)S(1)} collective-permute-done((f32[4,128,256]{1,0,2:T(4,128)S(1)}, f32[4,128,256]{1,0,2:T(4,128)S(1)}, u32[]{:S(2)}, u32[]{:S(2)}) %collective-permute-start) | collective-permute-done | bytes 524320 | tf_op jit(solution)/shard_map/while/body/eval_jaxpr/ppermute | solution.py:19
  456.8 1.0 constant_dynamic-slice_fusion.10
  457.9 1.9 collective-permute-start
  459.8 18.0 %collective-permute-done = f32[4,128,256]{1,0,2:T(4,128)S(1)} collective-permute-done((f32[4,128,256]{1,0,2:T(4,128)S(1)}, f32[4,128,256]{1,0,2:T(4,128)S(1)}, u32[]{:S(2)}, u32[]{:S(2)}) %collective-permute-start) | collective-permute-done | bytes 524320 | tf_op jit(solution)/shard_map/while/body/eval_jaxpr/ppermute | solution.py:19
  487.5 1.0 constant_dynamic-slice_fusion.10
  488.6 1.9 collective-permute-start
  490.5 17.0 %collective-permute-done = f32[4,128,256]{1,0,2:T(4,128)S(1)} collective-permute-done((f32[4,128,256]{1,0,2:T(4,128)S(1)}, f32[4,128,256]{1,0,2:T(4,128)S(1)}, u32[]{:S(2)}, u32[]{:S(2)}) %collective-permute-start) | collective-permute-done | bytes 524320 | tf_op jit(solution)/shard_map/while/body/eval_jaxpr/ppermute | solution.py:19
  517.3 1.0 constant_dynamic-slice_fusion.10
  518.4 1.9 collective-permute-start
  520.3 17.0 %collective-permute-done = f32[4,128,256]{1,0,2:T(4,128)S(1)} collective-permute-done((f32[4,128,256]{1,0,2:T(4,128)S(1)}, f32[4,128,256]{1,0,2:T(4,128)S(1)}, u32[]{:S(2)}, u32[]{:S(2)}) %collective-permute-start) | collective-permute-done | bytes 524320 | tf_op jit(solution)/shard_map/while/body/eval_jaxpr/ppermute | solution.py:19
  547.1 1.0 constant_dynamic-slice_fusion.10
  548.2 1.9 collective-permute-start
  550.1 17.0 %collective-permute-done = f32[4,128,256]{1,0,2:T(4,128)S(1)} collective-permute-done((f32[4,128,256]{1,0,2:T(4,128)S(1)}, f32[4,128,256]{1,0,2:T(4,128)S(1)}, u32[]{:S(2)}, u32[]{:S(2)}) %collective-permute-start) | collective-permute-done | bytes 524320 | tf_op jit(solution)/shard_map/while/body/eval_jaxpr/ppermute | solution.py:19
  576.8 1.0 constant_dynamic-slice_fusion.10
  577.9 1.9 collective-permute-start
  579.9 17.0 %collective-permute-done = f32[4,128,256]{1,0,2:T(4,128)S(1)} collective-permute-done((f32[4,128,256]{1,0,2:T(4,128)S(1)}, f32[4,128,256]{1,0,2:T(4,128)S(1)}, u32[]{:S(2)}, u32[]{:S(2)}) %collective-permute-start) | collective-permute-done | bytes 524320 | tf_op jit(solution)/shard_map/while/body/eval_jaxpr/ppermute | solution.py:19
  607.7 1.9 collective-permute-start
  609.6 17.0 %collective-permute-done = f32[4,128,256]{1,0,2:T(4,128)S(1)} collective-permute-done((f32[4,128,256]{1,0,2:T(4,128)S(1)}, f32[4,128,256]{1,0,2:T(4,128)S(1)}, u32[]{:S(2)}, u32[]{:S(2)}) %collective-permute-start) | collective-permute-done | bytes 524320 | tf_op jit(solution)/shard_map/while/body/eval_jaxpr/ppermute | solution.py:19
  636.4 1.0 constant_dynamic-slice_fusion.10
  637.5 1.9 collective-permute-start
  639.4 17.0 %collective-permute-done = f32[4,128,256]{1,0,2:T(4,128)S(1)} collective-permute-done((f32[4,128,256]{1,0,2:T(4,128)S(1)}, f32[4,128,256]{1,0,2:T(4,128)S(1)}, u32[]{:S(2)}, u32[]{:S(2)}) %collective-permute-start) | collective-permute-done | bytes 524320 | tf_op jit(solution)/shard_map/while/body/eval_jaxpr/ppermute | solution.py:19
  666.2 1.0 constant_dynamic-slice_fusion.10
  667.3 1.9 collective-permute-start
  669.2 17.0 %collective-permute-done = f32[4,128,256]{1,0,2:T(4,128)S(1)} collective-permute-done((f32[4,128,256]{1,0,2:T(4,128)S(1)}, f32[4,128,256]{1,0,2:T(4,128)S(1)}, u32[]{:S(2)}, u32[]{:S(2)}) %collective-permute-start) | collective-permute-done | bytes 524320 | tf_op jit(solution)/shard_map/while/body/eval_jaxpr/ppermute | solution.py:19
  697.0 1.9 collective-permute-start
  699.0 17.0 %collective-permute-done = f32[4,128,256]{1,0,2:T(4,128)S(1)} collective-permute-done((f32[4,128,256]{1,0,2:T(4,128)S(1)}, f32[4,128,256]{1,0,2:T(4,128)S(1)}, u32[]{:S(2)}, u32[]{:S(2)}) %collective-permute-start) | collective-permute-done | bytes 524320 | tf_op jit(solution)/shard_map/while/body/eval_jaxpr/ppermute | solution.py:19
  726.8 1.9 collective-permute-start
  728.7 17.0 %collective-permute-done = f32[4,128,256]{1,0,2:T(4,128)S(1)} collective-permute-done((f32[4,128,256]{1,0,2:T(4,128)S(1)}, f32[4,128,256]{1,0,2:T(4,128)S(1)}, u32[]{:S(2)}, u32[]{:S(2)}) %collective-permute-start) | collective-permute-done | bytes 524320 | tf_op jit(solution)/shard_map/while/body/eval_jaxpr/ppermute | solution.py:19
  756.6 1.9 collective-permute-start
  758.5 17.0 %collective-permute-done = f32[4,128,256]{1,0,2:T(4,128)S(1)} collective-permute-done((f32[4,128,256]{1,0,2:T(4,128)S(1)}, f32[4,128,256]{1,0,2:T(4,128)S(1)}, u32[]{:S(2)}, u32[]{:S(2)}) %collective-permute-start) | collective-permute-done | bytes 524320 | tf_op jit(solution)/shard_map/while/body/eval_jaxpr/ppermute | solution.py:19
  775.6 18.7 %collective-permute-start.1 = (f32[128,256]{0,1:T(8,128)S(1)}, f32[128,256]{0,1:T(8,128)S(1)}, u32[]{:S(2)}, u32[]{:S(2)}) collective-permute-start(f32[128,256]{0,1:T(8,128)S(1)} %slice_bitcast_fusion.2), channel_id=1, source_target_pairs={{8,0},{16,8},{24,16},{32,24},{40,32},{48,40},{56,48},{64,56},{72,6... | collective-permute-start | bytes 393224 | tf_op jit(solution)/shard_map/ppermute | solution.py:25
  794.5 2.7 collective-permute-done.1
  797.2 1.9 collective-permute-start.2
  799.3 4.2 collective-permute-done.2
  803.5 1.9 collective-permute-start.3
  805.9 4.0 collective-permute-done.3
  811.1 138.8 %all-reduce.2.cloned.1.call-done = f32[128,256]{0,1:T(8,128)} async-done(((f32[128,256]{0,1:T(8,128)}), f32[128,256]{0,1:T(8,128)}) %all-reduce.2.cloned.1.call-update) | async-done | bytes 131088 | tf_op jit(solution)/shard_map/psum | solution.py:220
  951.7 1.1 convolution_bitcast_fusion
  953.8 115.3 %all-gather.9.cloned.1.call-done = f32[64,3,1536]{2,1,0:T(4,128)} async-done(((f32[1,3,1536]{2,1,0:T(4,128)}), f32[64,3,1536]{2,1,0:T(4,128)}) %all-gather.9.cloned.1.call-update) | async-done | bytes 1179664 | tf_op jit(solution)/shard_map/all_gather | solution.py:240
  1069.1 1.8 reshape.271
  (340 shorter events, 44.5 us)
Async XLA Ops:
  6.5 8.6 copy-start
  6.5 129.4 %all-gather.5.cloned.1.call-start = ((), (), s32[]{:S(2)}) async-start(), calls=%async_computation | async-start | bytes 2129920 | tf_op jit(solution)/shard_map/all_gather | solution.py:70
  7.3 247.3 %all-gather.7.cloned.1.call-start = ((), (), s32[]{:S(2)}) async-start(), calls=%async_computation.1 | async-start | bytes 2129920 | tf_op jit(solution)/shard_map/all_gather | solution.py:71
  8.0 941.9 %all-reduce.2.cloned.1.call-start = ((), (), s32[]{:S(2)}) async-start(), calls=%async_computation.2 | async-start | bytes 262144 | tf_op jit(solution)/shard_map/psum | solution.py:220
  270.4 44.5 %collective-permute-start = (f32[4,128,256]{1,0,2:T(4,128)S(1)}, f32[4,128,256]{1,0,2:T(4,128)S(1)}, u32[]{:S(2)}, u32[]{:S(2)}) collective-permute-start(f32[4,128,256]{1,0,2:T(4,128)S(1)} %get-tuple-element.1388), channel_id=1, source_target_pairs={{0,32},{8,40},{16,48},{24,56},{32,64},{40,72},{48,80},{56,88},{64,... | collective-permute-start | bytes 1572872 | tf_op jit(solution)/shard_map/while/body/eval_jaxpr/ppermute | solution.py:19
  325.7 23.6 %collective-permute-start = (f32[4,128,256]{1,0,2:T(4,128)S(1)}, f32[4,128,256]{1,0,2:T(4,128)S(1)}, u32[]{:S(2)}, u32[]{:S(2)}) collective-permute-start(f32[4,128,256]{1,0,2:T(4,128)S(1)} %get-tuple-element.1388), channel_id=1, source_target_pairs={{0,32},{8,40},{16,48},{24,56},{32,64},{40,72},{48,80},{56,88},{64,... | collective-permute-start | bytes 1572872 | tf_op jit(solution)/shard_map/while/body/eval_jaxpr/ppermute | solution.py:19
  360.1 22.7 %collective-permute-start = (f32[4,128,256]{1,0,2:T(4,128)S(1)}, f32[4,128,256]{1,0,2:T(4,128)S(1)}, u32[]{:S(2)}, u32[]{:S(2)}) collective-permute-start(f32[4,128,256]{1,0,2:T(4,128)S(1)} %get-tuple-element.1388), channel_id=1, source_target_pairs={{0,32},{8,40},{16,48},{24,56},{32,64},{40,72},{48,80},{56,88},{64,... | collective-permute-start | bytes 1572872 | tf_op jit(solution)/shard_map/while/body/eval_jaxpr/ppermute | solution.py:19
  393.6 21.7 %collective-permute-start = (f32[4,128,256]{1,0,2:T(4,128)S(1)}, f32[4,128,256]{1,0,2:T(4,128)S(1)}, u32[]{:S(2)}, u32[]{:S(2)}) collective-permute-start(f32[4,128,256]{1,0,2:T(4,128)S(1)} %get-tuple-element.1388), channel_id=1, source_target_pairs={{0,32},{8,40},{16,48},{24,56},{32,64},{40,72},{48,80},{56,88},{64,... | collective-permute-start | bytes 1572872 | tf_op jit(solution)/shard_map/while/body/eval_jaxpr/ppermute | solution.py:19
  426.2 20.8 %collective-permute-start = (f32[4,128,256]{1,0,2:T(4,128)S(1)}, f32[4,128,256]{1,0,2:T(4,128)S(1)}, u32[]{:S(2)}, u32[]{:S(2)}) collective-permute-start(f32[4,128,256]{1,0,2:T(4,128)S(1)} %get-tuple-element.1388), channel_id=1, source_target_pairs={{0,32},{8,40},{16,48},{24,56},{32,64},{40,72},{48,80},{56,88},{64,... | collective-permute-start | bytes 1572872 | tf_op jit(solution)/shard_map/while/body/eval_jaxpr/ppermute | solution.py:19
  457.9 19.9 %collective-permute-start = (f32[4,128,256]{1,0,2:T(4,128)S(1)}, f32[4,128,256]{1,0,2:T(4,128)S(1)}, u32[]{:S(2)}, u32[]{:S(2)}) collective-permute-start(f32[4,128,256]{1,0,2:T(4,128)S(1)} %get-tuple-element.1388), channel_id=1, source_target_pairs={{0,32},{8,40},{16,48},{24,56},{32,64},{40,72},{48,80},{56,88},{64,... | collective-permute-start | bytes 1572872 | tf_op jit(solution)/shard_map/while/body/eval_jaxpr/ppermute | solution.py:19
  488.6 18.9 %collective-permute-start = (f32[4,128,256]{1,0,2:T(4,128)S(1)}, f32[4,128,256]{1,0,2:T(4,128)S(1)}, u32[]{:S(2)}, u32[]{:S(2)}) collective-permute-start(f32[4,128,256]{1,0,2:T(4,128)S(1)} %get-tuple-element.1388), channel_id=1, source_target_pairs={{0,32},{8,40},{16,48},{24,56},{32,64},{40,72},{48,80},{56,88},{64,... | collective-permute-start | bytes 1572872 | tf_op jit(solution)/shard_map/while/body/eval_jaxpr/ppermute | solution.py:19
  518.4 18.9 %collective-permute-start = (f32[4,128,256]{1,0,2:T(4,128)S(1)}, f32[4,128,256]{1,0,2:T(4,128)S(1)}, u32[]{:S(2)}, u32[]{:S(2)}) collective-permute-start(f32[4,128,256]{1,0,2:T(4,128)S(1)} %get-tuple-element.1388), channel_id=1, source_target_pairs={{0,32},{8,40},{16,48},{24,56},{32,64},{40,72},{48,80},{56,88},{64,... | collective-permute-start | bytes 1572872 | tf_op jit(solution)/shard_map/while/body/eval_jaxpr/ppermute | solution.py:19
  548.2 18.9 %collective-permute-start = (f32[4,128,256]{1,0,2:T(4,128)S(1)}, f32[4,128,256]{1,0,2:T(4,128)S(1)}, u32[]{:S(2)}, u32[]{:S(2)}) collective-permute-start(f32[4,128,256]{1,0,2:T(4,128)S(1)} %get-tuple-element.1388), channel_id=1, source_target_pairs={{0,32},{8,40},{16,48},{24,56},{32,64},{40,72},{48,80},{56,88},{64,... | collective-permute-start | bytes 1572872 | tf_op jit(solution)/shard_map/while/body/eval_jaxpr/ppermute | solution.py:19
  577.9 18.9 %collective-permute-start = (f32[4,128,256]{1,0,2:T(4,128)S(1)}, f32[4,128,256]{1,0,2:T(4,128)S(1)}, u32[]{:S(2)}, u32[]{:S(2)}) collective-permute-start(f32[4,128,256]{1,0,2:T(4,128)S(1)} %get-tuple-element.1388), channel_id=1, source_target_pairs={{0,32},{8,40},{16,48},{24,56},{32,64},{40,72},{48,80},{56,88},{64,... | collective-permute-start | bytes 1572872 | tf_op jit(solution)/shard_map/while/body/eval_jaxpr/ppermute | solution.py:19
  607.7 18.9 %collective-permute-start = (f32[4,128,256]{1,0,2:T(4,128)S(1)}, f32[4,128,256]{1,0,2:T(4,128)S(1)}, u32[]{:S(2)}, u32[]{:S(2)}) collective-permute-start(f32[4,128,256]{1,0,2:T(4,128)S(1)} %get-tuple-element.1388), channel_id=1, source_target_pairs={{0,32},{8,40},{16,48},{24,56},{32,64},{40,72},{48,80},{56,88},{64,... | collective-permute-start | bytes 1572872 | tf_op jit(solution)/shard_map/while/body/eval_jaxpr/ppermute | solution.py:19
  637.5 18.9 %collective-permute-start = (f32[4,128,256]{1,0,2:T(4,128)S(1)}, f32[4,128,256]{1,0,2:T(4,128)S(1)}, u32[]{:S(2)}, u32[]{:S(2)}) collective-permute-start(f32[4,128,256]{1,0,2:T(4,128)S(1)} %get-tuple-element.1388), channel_id=1, source_target_pairs={{0,32},{8,40},{16,48},{24,56},{32,64},{40,72},{48,80},{56,88},{64,... | collective-permute-start | bytes 1572872 | tf_op jit(solution)/shard_map/while/body/eval_jaxpr/ppermute | solution.py:19
  667.3 18.9 %collective-permute-start = (f32[4,128,256]{1,0,2:T(4,128)S(1)}, f32[4,128,256]{1,0,2:T(4,128)S(1)}, u32[]{:S(2)}, u32[]{:S(2)}) collective-permute-start(f32[4,128,256]{1,0,2:T(4,128)S(1)} %get-tuple-element.1388), channel_id=1, source_target_pairs={{0,32},{8,40},{16,48},{24,56},{32,64},{40,72},{48,80},{56,88},{64,... | collective-permute-start | bytes 1572872 | tf_op jit(solution)/shard_map/while/body/eval_jaxpr/ppermute | solution.py:19
  697.0 18.9 %collective-permute-start = (f32[4,128,256]{1,0,2:T(4,128)S(1)}, f32[4,128,256]{1,0,2:T(4,128)S(1)}, u32[]{:S(2)}, u32[]{:S(2)}) collective-permute-start(f32[4,128,256]{1,0,2:T(4,128)S(1)} %get-tuple-element.1388), channel_id=1, source_target_pairs={{0,32},{8,40},{16,48},{24,56},{32,64},{40,72},{48,80},{56,88},{64,... | collective-permute-start | bytes 1572872 | tf_op jit(solution)/shard_map/while/body/eval_jaxpr/ppermute | solution.py:19
  726.8 18.9 %collective-permute-start = (f32[4,128,256]{1,0,2:T(4,128)S(1)}, f32[4,128,256]{1,0,2:T(4,128)S(1)}, u32[]{:S(2)}, u32[]{:S(2)}) collective-permute-start(f32[4,128,256]{1,0,2:T(4,128)S(1)} %get-tuple-element.1388), channel_id=1, source_target_pairs={{0,32},{8,40},{16,48},{24,56},{32,64},{40,72},{48,80},{56,88},{64,... | collective-permute-start | bytes 1572872 | tf_op jit(solution)/shard_map/while/body/eval_jaxpr/ppermute | solution.py:19
  756.6 18.9 %collective-permute-start = (f32[4,128,256]{1,0,2:T(4,128)S(1)}, f32[4,128,256]{1,0,2:T(4,128)S(1)}, u32[]{:S(2)}, u32[]{:S(2)}) collective-permute-start(f32[4,128,256]{1,0,2:T(4,128)S(1)} %get-tuple-element.1388), channel_id=1, source_target_pairs={{0,32},{8,40},{16,48},{24,56},{32,64},{40,72},{48,80},{56,88},{64,... | collective-permute-start | bytes 1572872 | tf_op jit(solution)/shard_map/while/body/eval_jaxpr/ppermute | solution.py:19
  775.6 21.6 %collective-permute-start.1 = (f32[128,256]{0,1:T(8,128)S(1)}, f32[128,256]{0,1:T(8,128)S(1)}, u32[]{:S(2)}, u32[]{:S(2)}) collective-permute-start(f32[128,256]{0,1:T(8,128)S(1)} %slice_bitcast_fusion.2), channel_id=1, source_target_pairs={{8,0},{16,8},{24,16},{32,24},{40,32},{48,40},{56,48},{64,56},{72,6... | collective-permute-start | bytes 393224 | tf_op jit(solution)/shard_map/ppermute | solution.py:25
  797.2 6.3 collective-permute-start.2
  799.2 153.7 %copy-start.1 = (s32[64]{0:T(128)S(1)}, s32[64]{0:T(128)}, u32[]{:S(2)}) copy-start(s32[64]{0:T(128)} %param.34) | copy-start | bytes 772
  799.2 154.1 %copy-start.2 = (s32[64]{0:T(128)S(1)}, s32[64]{0:T(128)}, u32[]{:S(2)}) copy-start(s32[64]{0:T(128)} %param.35) | copy-start | bytes 772
  803.5 6.3 collective-permute-start.3
  811.0 258.1 %all-gather.9.cloned.1.call-start = ((), (), s32[]{:S(2)}) async-start(), calls=%async_computation.3 | async-start | bytes 1597440 | tf_op jit(solution)/shard_map/all_gather | solution.py:240
Sparse Core Ops, SparseCore 0:
  9.5 126.3 all-gather.4
  138.1 116.4 all-gather.6
  811.2 138.7 all-reduce.1
  953.0 116.1 all-gather.8
where the time goes:
time: 1080 us
  waiting for transfers between devices  812 us (75%)
  loops' own time  138 us (13%)
  starting transfers between devices  56 us (5%)
  local copies, waits for them, and re-layouts  36.2 us (3%)
  other arithmetic  16 us (1%)
  between operations  13.4 us (1%)
    ppermute x16, waiting for transfers between devices, from_behind(): return lax.ppermute(value, axis, pairs)  309 us
    psum x1, waiting for transfers between devices, on_device(): lax.psum(jnp.concatenate([input_part, grad_parts], axis=1).reshape(-1), '...  139 us
    another operation x1, loops' own time, on_device(): lax.fori_loop(0, seq_count // 4, backward_step, (initial_couriers, jnp.ze...  135 us
    all_gather x1, waiting for transfers between devices, on_device(): lax.all_gather(key_states, 'seq', axis=0, tiled=True)  120 us
    all_gather x1, waiting for transfers between devices, on_device(): lax.all_gather(value_states, 'seq', axis=0, tiled=True)  116 us
    all_gather x1, waiting for transfers between devices, on_device(): everyone = lax.all_gather(partials, 'seq', axis=0, tiled=True)  115 us
    ppermute x16, starting transfers between devices, from_behind(): return lax.ppermute(value, axis, pairs)  33.3 us
    ppermute x3, starting transfers between devices, from_behind_2(): lax.ppermute(value, axis, [(source, source + steps) for source in range(i...  22.6 us
  transfers between devices with their start and end apart: 23, of which 23 were waited for; matrix products, arithmetic and copies ran while one was open for 1% of the time, Pallas kernels for 0%

commit v1 on v0

v1 whole, which is shorter than its diff:
```python
import functools
import math

import jax
import jax.numpy as jnp
from jax import lax
from jax.experimental import pallas as pl
from jax.experimental.pallas import tpu as pltpu
from jax.sharding import PartitionSpec as P

SEQ_GRID = (8, 4, 2)
HEAD_GRID = (4, 2)

T = 128
F = 128
H = 4
SK = 64
GROUP = 4
DOCS_MOST = 8
LOW = -1e30
MESH = pl.DeviceIdType.MESH
F32 = jnp.float32
BF16 = jnp.bfloat16


def dot_nt(a, b):
    return lax.dot_general(a, b, (((1,), (1,)), ((), ())), preferred_element_type=F32)


def dot_nn(a, b):
    return jnp.dot(a, b, preferred_element_type=F32)


def sign_table(hashes):
    buckets = lax.broadcasted_iota(jnp.int32, (SK, hashes.shape[1]), 0)
    signs = (1 - 2 * (hashes[1:2, :] & 1)).astype(F32)
    return jnp.where(buckets == hashes[0:1, :], signs, 0.0).astype(BF16)


def rem(value, count):
    return lax.rem(value + count, count)


class Place:
    def __init__(self):
        self.planes, self.chips, self.cores = SEQ_GRID
        self.ys, self.halves = HEAD_GRID
        self.width = self.chips * self.cores
        seq = lax.axis_index("seq")
        head = lax.axis_index("head")
        self.seq, self.head = seq, head
        self.i = lax.rem(seq, self.width)
        self.z = seq // self.width
        self.c = lax.rem(self.i, self.cores)
        self.x = self.i // self.cores
        self.y = head // self.halves
        self.half = lax.rem(head, self.halves)

    def at(self, z=None, i=None, y=None, half=None):
        z = self.z if z is None else z
        i = self.i if i is None else i
        y = self.y if y is None else y
        half = self.half if half is None else half
        return (z * self.width + i, y * self.halves + half)


def remote(src, dst, send_sem, recv_sem, device):
    return pltpu.make_async_remote_copy(
        src_ref=src, dst_ref=dst, send_sem=send_sem, recv_sem=recv_sem, device_id=device, device_id_type=MESH
    )


def meet(devices):
    barrier = pltpu.get_barrier_semaphore()
    for device in devices:
        pl.semaphore_signal(barrier, inc=1, device_id=device, device_id_type=MESH)
    pl.semaphore_wait(barrier, len(devices))


def attention_kernel(
    x_ref, q_ref, k_ref, v_ref, do_ref, xh_ref, qh_ref, kh_ref, vh_ref,
    input_out, grad_out,
    qall, kv, scores, wgrads, stat, kmt, stat_send, stat_recv, fin, total, dq_acc, dkv_acc,
    dkv_send, dkv_recv, dq_send, dq_recv, iy, iz,
    q_recv, q_own, q_ring, q_sib, kv_send_sem, kv_recv_sem, st_send_sem, st_recv_sem, fin_send_sem, fin_recv_sem,
    dkv_send_sem, dkv_recv_sem, dq_send_sem, dq_recv_sem, iy_send_sem, iy_recv_sem, iz_send_sem, iz_recv_sem,
):
    me = Place()
    planes, chips, width = me.planes, me.chips, me.width
    x, c, z, i = me.x, me.c, me.z, me.i
    rows = 2 * T
    scale = 1.0 / math.sqrt(F)
    scale2 = scale * math.log2(math.e)

    mine = pl.ds(pl.multiple_of(c * T, T), T)
    other = pl.ds(pl.multiple_of((1 - c) * T, T), T)
    for h in range(H):
        qall[x, 0, h, mine, :] = q_ref[:, h * F:(h + 1) * F]
        qall[x, 1, h, mine, :] = do_ref[:, h * F:(h + 1) * F]
    kv[z, 0] = k_ref[...]
    kv[z, 1] = v_ref[...]

    peers = [me.at(i=rem(i + o, width)) for o in range(1, width)]
    friends = peers + [me.at(z=rem(z + o, planes)) for o in range(1, planes)]
    friends += [me.at(y=rem(me.y + o, me.ys)) for o in range(1, me.ys)]
    friends += [me.at(half=1 - me.half)] if me.halves > 1 else []
    meet(friends)

    def piece(step, core, part):
        s = rem(x + step, chips)
        ref = qall.at[s, part, :, pl.ds(pl.multiple_of(core * T, T), T), :]
        return ref, q_recv.at[s, core, part]

    def send_piece(step, core, part, send_sem, target):
        ref, recv_sem = piece(step, core, part)
        return remote(ref, ref, send_sem, recv_sem, target)

    sibling = me.at(i=x * 2 + 1 - c)
    right = me.at(i=rem(x + 1, chips) * 2 + c)
    left = me.at(i=rem(x + chips - 1, chips) * 2 + c)
    own_copies = [
        send_piece(0, c, part, q_own.at[n, part], target)
        for n, target in enumerate((sibling, right, left)) for part in range(2)
    ]
    ring_copies = [
        send_piece(chips - 1, c, 0, q_ring.at[0], right),
        send_piece(1, c, 1, q_ring.at[1], left),
    ]
    sib_copies = {
        (step, part): send_piece(step, c, part, q_sib.at[step - 1, part], sibling)
        for step in (1, 2, 3) for part in range(2)
    }

    def wait_piece(step, core, part):
        ref, recv_sem = piece(step, core, part)
        remote(ref, ref, q_own.at[0, 0], recv_sem, sibling).wait_recv()

    def kv_copy(b):
        return remote(kv.at[b], kv.at[b], kv_send_sem.at[b], kv_recv_sem.at[b], me.at(z=rem(z + 1, planes)))

    has_above = z < planes - 1

    @pl.when(has_above)
    def _():
        kv_copy(z).start()

    for copy in own_copies:
        copy.start()

    input_part = dot_nt(sign_table(xh_ref[...]), x_ref[...])
    iy[me.y] = input_part.astype(BF16)
    iy_copies = [
        remote(iy.at[me.y], iy.at[me.y], iy_send_sem.at[o - 1], iy_recv_sem.at[me.y], me.at(y=rem(me.y + o, me.ys)))
        for o in range(1, me.ys)
    ]
    for copy in iy_copies:
        copy.start()
    iz_copy = remote(iz.at[me.half], iz.at[me.half], iz_send_sem.at[0], iz_recv_sem.at[me.half], me.at(half=1 - me.half))

    def input_over_y():
        for o in range(1, me.ys):
            y = rem(me.y + o, me.ys)
            remote(iy.at[y], iy.at[y], iy_send_sem.at[0], iy_recv_sem.at[y], me.at(y=y)).wait_recv()
        summed = iy[0].astype(F32)
        for y in range(1, me.ys):
            summed = summed + iy[y].astype(F32)
        iz[me.half] = summed.astype(BF16)
        if me.halves > 1:
            iz_copy.start()

    query_table = sign_table(qh_ref[...])
    query_tables = jnp.concatenate([query_table[:, h * F:(h + 1) * F] for h in range(H)], axis=0)
    key_table = sign_table(kh_ref[...])
    value_table = sign_table(vh_ref[...])

    for s in range(chips):
        stat[s, 0:1, :] = jnp.full((1, H * rows), LOW, F32)
        stat[s, 1:3, :] = jnp.zeros((2, H * rows), F32)

    def first_unit(s, k, masked):
        b = z - k
        for h in range(H):
            cols = pl.ds(h * rows, rows)
            st = dot_nt(kv[b, 0], qall[s, 0, h]) * scale2
            if masked:
                key_place = lax.broadcasted_iota(jnp.int32, (T, rows), 0) + i * T
                query_place = lax.broadcasted_iota(jnp.int32, (T, rows), 1) + s * rows
                st = jnp.where(key_place <= query_place, st, LOW)
            dp = dot_nt(kv[b, 1], qall[s, 1, h])
            scores[s, k, :, cols] = st
            wgrads[s, k, :, cols] = dp
            old_top = stat[s, 0:1, cols]
            top = jnp.maximum(old_top, jnp.max(st, axis=0, keepdims=True))
            e = jnp.exp2(st - top)
            keep = jnp.exp2(old_top - top)
            stat[s, 0:1, cols] = top
            stat[s, 1:2, cols] = stat[s, 1:2, cols] * keep + jnp.sum(e, axis=0, keepdims=True)
            stat[s, 2:3, cols] = stat[s, 2:3, cols] * keep + jnp.sum(e * dp, axis=0, keepdims=True)

    def first_step(t, carry):
        @pl.when(jnp.logical_and(t >= 1, t <= z))
        def _():
            kv_copy(z - t).wait_recv()

            @pl.when(has_above)
            def _():
                kv_copy(z - t).start()

        @pl.when(t <= z)
        def _():
            kmt[t] = dot_nt(query_tables, kv[z - t, 0]).astype(BF16)

        @pl.when(t == 0)
        def _():
            for part in range(2):
                wait_piece(0, 1 - c, part)

        @pl.when(t == 2)
        def _():
            for step in (chips - 1, 1):
                for part in range(2):
                    wait_piece(step, c, part)
                    sib_copies[(step, part)].start()
                ring_copies[0 if step == chips - 1 else 1].start()

        @pl.when(t == 3)
        def _():
            for step in (chips - 1, 1):
                for part in range(2):
                    wait_piece(step, 1 - c, part)
            input_over_y()

        @pl.when(t == 5)
        def _():
            for part in range(2):
                wait_piece(2, c, part)
                sib_copies[(2, part)].start()

        @pl.when(t == 6)
        def _():
            for part in range(2):
                wait_piece(2, 1 - c, part)

        def over_chips(r, carry):
            s = rem(x + r * (r + 1) // 2, chips)
            active = 3 * ((r + 1) // 2)
            low = jnp.where(t == active, 0, t)
            high = jnp.where(t >= active, jnp.minimum(t, z) + 1, 0)

            @pl.when(jnp.logical_and(low == 0, high > 0))
            def _():
                first_unit(s, 0, True)

            def over_blocks(k, carry):
                first_unit(s, k, False)
                return carry

            return lax.fori_loop(jnp.maximum(low, 1), high, over_blocks, carry)

        return lax.fori_loop(0, chips, over_chips, carry)

    lax.fori_loop(0, 8, first_step, 0)

    for s in range(chips):
        for core in range(2):
            for h in range(H):
                first = h * rows + core * T
                stat_send[s * 2 + core, 0:3, h * T:(h + 1) * T] = stat[s, 0:3, first:first + T]
    st_copies = [
        remote(
            stat_send.at[rem(i + o, width)], stat_recv.at[i], st_send_sem.at[o - 1], st_recv_sem.at[i],
            me.at(i=rem(i + o, width)),
        )
        for o in range(1, width)
    ]
    for copy in st_copies:
        copy.start()
    stat_recv[i] = stat_send[i]
    for o in range(1, width):
        p = rem(i + o, width)
        remote(stat_send.at[p], stat_recv.at[p], st_send_sem.at[0], st_recv_sem.at[p], me.at(i=p)).wait_recv()
    top = stat_recv[0, 0:1, :]
    for p in range(1, width):
        top = jnp.maximum(top, stat_recv[p, 0:1, :])
    weight_sum = jnp.zeros_like(top)
    delta_sum = jnp.zeros_like(top)
    for p in range(width):
        factor = jnp.exp2(stat_recv[p, 0:1, :] - top)
        weight_sum = weight_sum + stat_recv[p, 1:2, :] * factor
        delta_sum = delta_sum + stat_recv[p, 2:3, :] * factor
    fin[i, 0:1, :] = top + jnp.log2(weight_sum)
    fin[i, 1:2, :] = delta_sum / weight_sum
    fin_copies = [
        remote(fin.at[i], fin.at[i], fin_send_sem.at[o - 1], fin_recv_sem.at[i], me.at(i=rem(i + o, width)))
        for o in range(1, width)
    ]
    for copy in fin_copies:
        copy.start()
    dq_acc[...] = jnp.zeros_like(dq_acc)
    for o in range(1, width):
        p = rem(i + o, width)
        remote(fin.at[p], fin.at[p], fin_send_sem.at[0], fin_recv_sem.at[p], me.at(i=p)).wait_recv()
    for s in range(chips):
        for core in range(2):
            for h in range(H):
                first = h * rows + core * T
                total[s, 0:2, first:first + T] = fin[s * 2 + core, 0:2, h * T:(h + 1) * T]

    def second_unit(s, k):
        lows, grads = [], []
        for h in range(H):
            cols = pl.ds(h * rows, rows)
            p = jnp.exp2(scores[s, k, :, cols] - total[s, 0:1, cols])
            g = p * (wgrads[s, k, :, cols] - total[s, 1:2, cols])
            lows.append(p.astype(BF16))
            g = g.astype(BF16)
            grads.append(g)
            dq_acc[s] += dot_nn(kmt[k, h * SK:(h + 1) * SK, :], g)
        low = jnp.concatenate(lows, axis=1)
        grad = jnp.concatenate(grads, axis=1)
        dkv_acc[0] += dot_nn(grad, qall[s, 0].reshape(H * rows, F))
        dkv_acc[1] += dot_nn(low, qall[s, 1].reshape(H * rows, F))

    def dkv_copy(k, b):
        return remote(dkv_send.at[k], dkv_recv.at[z], dkv_send_sem.at[k], dkv_recv_sem.at[z], me.at(z=b))

    def second_step(n, carry):
        k = z - n
        dkv_acc[...] = jnp.zeros_like(dkv_acc)

        def over_chips(s, carry):
            second_unit(s, k)
            return carry

        lax.fori_loop(0, chips, over_chips, 0)
        dkv_send[k, 0:SK, :] = dot_nt(key_table, (dkv_acc[0] * scale).astype(BF16)).astype(BF16)
        dkv_send[k, SK:, :] = dot_nt(value_table, dkv_acc[1].astype(BF16)).astype(BF16)

        @pl.when(k > 0)
        def _():
            dkv_copy(k, n).start()

        return carry

    lax.fori_loop(0, z + 1, second_step, 0)

    for s in range(chips):
        for core in range(2):
            dq_send[s * 2 + core] = (dq_acc[s, :, core * T:(core + 1) * T] * scale).astype(BF16)
    dq_copies = [
        remote(
            dq_send.at[rem(i + o, width)], dq_recv.at[i], dq_send_sem.at[o - 1], dq_recv_sem.at[i],
            me.at(i=rem(i + o, width)),
        )
        for o in range(1, width)
    ]
    for copy in dq_copies:
        copy.start()

    if me.halves > 1:
        away = 1 - me.half
        remote(iz.at[away], iz.at[away], iz_send_sem.at[0], iz_recv_sem.at[away], me.at(half=away)).wait_recv()
    summed = iz[0].astype(F32)
    for half in range(1, me.halves):
        summed = summed + iz[half].astype(F32)
    input_out[...] = summed * math.sqrt(SK / (x_ref.shape[1] * me.ys * me.halves))

    heads = me.ys * me.halves
    kv_factor = math.sqrt(SK / (F * heads))
    grad_out[SK:3 * SK, :] = dkv_send[0].astype(F32) * kv_factor

    def add_kv(b, carry):
        remote(dkv_send.at[0], dkv_recv.at[b], dkv_send_sem.at[0], dkv_recv_sem.at[b], me.at(z=rem(z + 1, planes))).wait_recv()
        grad_out[SK:3 * SK, :] += dkv_recv[b].astype(F32) * kv_factor
        return carry

    dq_recv[i] = dq_send[i]
    lax.fori_loop(z + 1, planes, add_kv, 0)
    for o in range(1, width):
        p = rem(i + o, width)
        remote(dq_send.at[p], dq_recv.at[p], dq_send_sem.at[0], dq_recv_sem.at[p], me.at(i=p)).wait_recv()
    query_sum = dq_recv[0].astype(F32)
    for p in range(1, width):
        query_sum = query_sum + dq_recv[p].astype(F32)
    grad_out[0:SK, :] = query_sum * math.sqrt(SK / (H * F * heads))
    grad_out[3 * SK:, :] = jnp.zeros((SK, T), F32)

    for copy in own_copies + ring_copies + list(sib_copies.values()) + iy_copies + st_copies + fin_copies + dq_copies:
        copy.wait_send()
    if me.halves > 1:
        iz_copy.wait_send()

    @pl.when(has_above)
    def _():
        def left_kv(b, carry):
            kv_copy(b).wait_send()
            return carry

        lax.fori_loop(0, z + 1, left_kv, 0)

    def left_dkv(k, carry):
        dkv_copy(k, z - k).wait_send()
        return carry

    lax.fori_loop(1, z + 1, left_dkv, 0)


def attention(layer_input, queries, key_states, value_states, out_grad, input_hash, query_hash, key_hash, value_hash):
    planes, chips, cores = SEQ_GRID
    ys, halves = HEAD_GRID
    width = chips * cores
    rows = 2 * T
    dma = pltpu.SemaphoreType.DMA
    vmem = pltpu.VMEM
    return pl.pallas_call(
        attention_kernel,
        out_shape=(jax.ShapeDtypeStruct((SK, T), F32), jax.ShapeDtypeStruct((4 * SK, T), F32)),
        in_specs=[pl.BlockSpec(memory_space=pltpu.VMEM)] * 9,
        out_specs=(pl.BlockSpec(memory_space=pltpu.VMEM),) * 2,
        scratch_shapes=[
            vmem((chips, 2, H, rows, F), BF16),
            vmem((planes, 2, T, F), BF16),
            vmem((chips, planes, T, H * rows), F32),
            vmem((chips, planes, T, H * rows), F32),
            vmem((chips, 8, H * rows), F32),
            vmem((planes, H * SK, T), BF16),
            vmem((width, 8, H * T), F32),
            vmem((width, 8, H * T), F32),
            vmem((width, 8, H * T), F32),
            vmem((chips, 8, H * rows), F32),
            vmem((chips, SK, rows), F32),
            vmem((2, T, F), F32),
            vmem((planes, 2 * SK, T), BF16),
            vmem((planes, 2 * SK, T), BF16),
            vmem((width, SK, T), BF16),
            vmem((width, SK, T), BF16),
            vmem((ys, SK, T), BF16),
            vmem((halves, SK, T), BF16),
            dma((chips, 2, 2)), dma((3, 2)), dma((2,)), dma((3, 2)),
            dma((planes,)), dma((planes,)),
            dma((width,)), dma((width,)), dma((width,)), dma((width,)),
            dma((planes,)), dma((planes,)),
            dma((width,)), dma((width,)),
            dma((ys,)), dma((ys,)), dma((halves,)), dma((halves,)),
        ],
        compiler_params=pltpu.CompilerParams(
            collective_id=0, has_side_effects=True, vmem_limit_bytes=56 * 1024 * 1024
        ),
        name="attention_backward",
    )(layer_input, queries, key_states, value_states, out_grad, input_hash, query_hash, key_hash, value_hash)


def documents_kernel(
    starts, targets, input_ref, grad_ref, out_ref,
    products, near, plane_docs, far_send, far,
    near_send_sem, near_recv_sem, plane_send_sem, plane_recv_sem, far_send_sem, far_recv_sem,
):
    me = Place()
    planes, width, ys, halves = me.planes, me.width, me.ys, me.halves
    i, z = me.i, me.z
    doc_count = starts.shape[0]
    place_in_group = lax.rem(i, GROUP)
    group_first = i - place_in_group
    band = SK // ys
    line = planes * halves

    near_peers = []
    for o in range(1, GROUP * ys):
        p = rem(place_in_group + o // ys, GROUP)
        y = rem(me.y + o % ys, ys)
        near_peers.append((p, y))
    far_peers = []
    for o in range(1, line):
        fz = rem(z + o // halves, planes)
        half = rem(me.half + o % halves, halves)
        far_peers.append((fz, half))
    friends = [me.at(i=rem(i + o, width)) for o in range(1, width)]
    friends += [me.at(i=group_first + p, y=y) for n, (p, y) in enumerate(near_peers) if (n + 1) % ys]
    friends += [me.at(z=fz, half=half) for fz, half in far_peers]
    barrier = pltpu.get_barrier_semaphore()
    for device in friends:
        pl.semaphore_signal(barrier, inc=1, device_id=device, device_id_type=MESH)

    group_tokens = GROUP * T
    tokens = lax.broadcasted_iota(jnp.int32, (1, T), 1)
    here = tokens + me.seq * T
    here_group = (me.seq // GROUP) * group_tokens
    slot_group = (z * (width // GROUP) + tokens // (2 * GROUP)) * group_tokens
    doc_of = jnp.zeros((1, T), jnp.int32)
    slot_first = jnp.zeros((1, T), jnp.int32)
    slot_past = jnp.zeros((1, T), jnp.int32)
    for d in range(doc_count):
        begins = starts[d]
        doc_of = doc_of + jnp.where(jnp.logical_and(begins <= here, begins > here_group), 1, 0)
        slot_first = slot_first + jnp.where(begins < slot_group, 1, 0)
        slot_past = slot_past + jnp.where(begins < slot_group + group_tokens, 1, 0)
    slot_doc = slot_first + lax.rem(tokens, 2 * GROUP)
    slot_doc = jnp.where(slot_doc < slot_past, slot_doc, -1)
    slot_row = jnp.full((1, T), -1, jnp.int32)
    for d in range(doc_count):
        slot_row = jnp.where(slot_doc == d, targets[d], slot_row)

    input_sketch = input_ref[...]
    masked = jnp.concatenate([jnp.where(doc_of == e, input_sketch, 0.0) for e in range(DOCS_MOST)], axis=0)
    grads = grad_ref[...]
    masked_high = masked.astype(BF16)
    masked_low = (masked - masked_high.astype(F32)).astype(BF16)
    grads_high = grads.astype(BF16)
    grads_low = (grads - grads_high.astype(F32)).astype(BF16)
    product = dot_nt(masked_high, grads_high) + (dot_nt(masked_high, grads_low) + dot_nt(masked_low, grads_high))
    products[...] = product.reshape(DOCS_MOST, SK, 4 * SK).astype(BF16)

    pl.semaphore_wait(barrier, len(friends))

    def part(p, y):
        return products.at[pl.ds(p * 2, 2), pl.ds(pl.multiple_of(y * band, band), band), :]

    my_slot = place_in_group * ys + me.y
    near_copies = [
        remote(part(p, y), near.at[my_slot], near_send_sem.at[n], near_recv_sem.at[my_slot], me.at(i=group_first + p, y=y))
        for n, (p, y) in enumerate(near_peers)
    ]
    for copy in near_copies:
        copy.start()
    summed = part(place_in_group, me.y)[...].astype(F32)
    for p, y in near_peers:
        slot = p * ys + y
        remote(near.at[slot], near.at[slot], near_send_sem.at[0], near_recv_sem.at[slot], me.at(i=group_first + p, y=y)).wait_recv()
        summed = summed + near[slot].astype(F32)
    plane_docs[i] = summed.astype(BF16)

    plane_copies = [
        remote(plane_docs.at[i], plane_docs.at[i], plane_send_sem.at[o - 1], plane_recv_sem.at[i], me.at(i=rem(i + o, width)))
        for o in range(1, width)
    ]
    for copy in plane_copies:
        copy.start()
    for o in range(1, width):
        p = rem(i + o, width)
        remote(plane_docs.at[p], plane_docs.at[p], plane_send_sem.at[0], plane_recv_sem.at[p], me.at(i=p)).wait_recv()

    def gather_row(fz, carry):
        row = fz * width + i
        found = jnp.zeros((band, 4 * SK), F32)
        for j in range(width):
            for e in range(2):
                chosen = jnp.broadcast_to(slot_row[:, 2 * j + e:2 * j + e + 1], (band, 4 * SK)) == row
                found = found + jnp.where(chosen, plane_docs[j, e].astype(F32), 0.0)
        own = band // halves
        for half in range(halves):
            rows_half = found[half * own:(half + 1) * own, :]
            both = jnp.concatenate([rows_half[:, 0:2 * SK], rows_half[:, 2 * SK:]], axis=0)
            far_send[fz * halves + half] = both.astype(BF16)
        return carry

    lax.fori_loop(0, planes, gather_row, 0)
    my_line = z * halves + me.half
    far_copies = [
        remote(far_send.at[fz * halves + half], far.at[my_line], far_send_sem.at[n], far_recv_sem.at[my_line], me.at(z=fz, half=half))
        for n, (fz, half) in enumerate(far_peers)
    ]
    for copy in far_copies:
        copy.start()
    result = far_send[my_line].astype(F32)
    for fz, half in far_peers:
        slot = fz * halves + half
        remote(far.at[slot], far.at[slot], far_send_sem.at[0], far_recv_sem.at[slot], me.at(z=fz, half=half)).wait_recv()
        result = result + far[slot].astype(F32)
    own = band // halves
    out_ref[...] = jnp.concatenate([result[0:own], result[own:]], axis=1)

    for copy in near_copies + plane_copies + far_copies:
        copy.wait_send()


def documents(input_sketch, grad_sketch, doc_starts, doc_rows):
    planes, chips, cores = SEQ_GRID
    ys, halves = HEAD_GRID
    width = chips * cores
    line = planes * halves
    band = SK // ys
    dma = pltpu.SemaphoreType.DMA
    vmem = pltpu.VMEM
    return pl.pallas_call(
        documents_kernel,
        out_shape=jax.ShapeDtypeStruct((band // halves, 4 * SK), F32),
        in_specs=[pl.BlockSpec(memory_space=pltpu.SMEM)] * 2 + [pl.BlockSpec(memory_space=pltpu.VMEM)] * 2,
        out_specs=pl.BlockSpec(memory_space=pltpu.VMEM),
        scratch_shapes=[
            vmem((DOCS_MOST, SK, 4 * SK), BF16),
            vmem((GROUP * ys, 2, band, 4 * SK), BF16),
            vmem((width, 2, band, 4 * SK), BF16),
            vmem((line, 2 * band // halves, 2 * SK), BF16),
            vmem((line, 2 * band // halves, 2 * SK), BF16),
            dma((GROUP * ys,)), dma((GROUP * ys,)),
            dma((width,)), dma((width,)),
            dma((line,)), dma((line,)),
        ],
        compiler_params=pltpu.CompilerParams(collective_id=1, has_side_effects=True),
        name="documents",
    )(doc_starts, doc_rows, input_sketch, grad_sketch)


def on_device(
    layer_input, queries, key_states, value_states, out_grad,
    input_hash, query_hash, key_hash, value_hash, doc_starts, doc_rows,
):
    input_sketch, grad_sketch = attention(
        layer_input, queries, key_states, value_states, out_grad, input_hash, query_hash, key_hash, value_hash
    )
    result = documents(input_sketch, grad_sketch, doc_starts, doc_rows)
    bands = result.shape[0]
    return result[:, :3 * SK].reshape(bands, 3, SK).transpose(1, 0, 2).reshape(1, 3, bands * SK)


def solution(mesh):
    return jax.shard_map(
        on_device,
        mesh=mesh,
        in_specs=(
            P("seq", "head"), P("seq", "head"), P("seq", "head"), P("seq", "head"), P("seq", "head"),
            P(None, "head"), P(None, "head"), P(None, "head"), P(None, "head"),
            P(), P(),
        ),
        out_specs=P("seq", None, "head"),
        check_vma=False,
    )
```

time: 1080 us -> 97.7 us (0.09)
  waiting for transfers between devices: 812 us -> 0 us
  loops' own time: 138 us -> 0 us
  Pallas kernels: 0 us -> 96.1 us
  starting transfers between devices: 56 us -> 0 us
  local copies, waits for them, and re-layouts: 36.2 us -> 1.45 us
  other arithmetic: 16 us -> 0 us
  between operations: 13.4 us -> 0.02 us
    all_gather x3 -> x0, waiting for transfers between devices: 352 us -> none  [the longest x1 120 us: on_device(): lax.all_gather(key_states, 'seq', axis=0, tiled=True)]
    ppermute x19 -> x0, waiting for transfers between devices: 320 us -> none  [the longest x16 309 us: from_behind(): return lax.ppermute(value, axis, pairs)]
    psum x1 -> x0, waiting for transfers between devices: 139 us -> none  [on_device(): lax.psum(jnp.concatenate([input_part, grad_parts], axis=1).reshape(-1), '...]
    another operation x51 -> x0, loops' own time: 138 us -> none  [the longest x1 135 us: on_device(): lax.fori_loop(0, seq_count // 4, backward_step, (initial_couriers, jnp.ze...]
    pallas_call x0 -> x2, Pallas kernels: none -> 96.1 us  [the longest x1 62.3 us: attention(): pl.pallas_call(attention_kernel, out_shape=(jax.ShapeDtypeStruct((SK, T),...]
    ppermute x19 -> x0, starting transfers between devices: 55.9 us -> none  [the longest x16 33.3 us: from_behind(): return lax.ppermute(value, axis, pairs)]
    dynamic_slice x17 -> x0, local copies, waits for them, and re-layouts: 15.6 us -> none  [the longest x16 15.6 us: backward_step(): lax.dynamic_slice_in_dim(every_value_row, block_beginnings[courier_positi...]
    slice x21 -> x0, local copies, waits for them, and re-layouts: 13.2 us -> none  [the longest x16 9.87 us: backward_step(): block_beginnings[courier_position]]
  transfers between devices with their start and end apart: 23 -> 0, of which waited for: 23 -> 0; matrix products, arithmetic and copies ran while one was open for 1% -> 0% of each run, Pallas kernels for 0% -> 0%
where the time goes in v1:
time: 97.7 us; the launch traced here: 97.5 us
  Pallas kernels  96.1 us (98%)
  local copies, waits for them, and re-layouts  1.45 us (1%)
    pallas_call x1, Pallas kernels, attention(): pl.pallas_call(attention_kernel, out_shape=(jax.ShapeDtypeStruct((SK, T),...  62.3 us
    pallas_call x1, Pallas kernels, documents(): pl.pallas_call(documents_kernel, out_shape=jax.ShapeDtypeStruct((band //...  33.7 us

profile of v1, /device:TPU:1, one launch (start us, length us, event | category | flops | bytes accessed | tf_op | source)
XLA Modules:
  0.0 97.5 jit_solution(1696765264398132487)
XLA Ops:
  0.0 62.3 %attention_backward.1 = (f32[64,128]{1,0:T(8,128)}, f32[256,128]{1,0:T(8,128)}) custom-call(bf16[128,1024]{1,0:T(8,128)(2,1)} %x_ref.1, bf16[128,512]{1,0:T(8,128)(2,1)} %q_ref.1, bf16[128,128]{1,0:T(8,128)(2,1)} %k_ref.1, bf16[128,128]{1,0:T(8,128)(2,1)} %v_ref.1, bf16[128,512]{1,0:T(8,128)(2,1)} %do_ref.1, s32[2,1024]{1,0:T(2,128)} %xh_ref.1, ...), custom_call_target="tpu_custom_call" | custom-call | tf_op jit(solution)/shard_map/attention_backward/pallas_call | solution.py:415
  62.3 33.7 %documents.1 = f32[8,256]{1,0:T(8,128)} custom-call(s32[64]{0:T(128)} %starts.1, s32[64]{0:T(128)} %targets.1, f32[64,128]{1,0:T(8,128)} %get-tuple-element.7.input_ref, f32[256,128]{1,0:T(8,128)} %get-tuple-element.8.grad_ref), custom_call_target="tpu_custom_call" | custom-call | tf_op jit(solution)/shard_map/documents/pallas_call | solution.py:584
  96.1 0.8 reshape.6
  96.8 0.7 reshape.8
  (1 shorter events, 0.0 us)

commit v2 on v1

v2 whole, which is shorter than its diff:
```python
import functools
import math

import jax
import jax.numpy as jnp
from jax import lax
from jax.experimental import pallas as pl
from jax.experimental.pallas import tpu as pltpu
from jax.sharding import PartitionSpec as P

SEQ_GRID = (8, 4, 2)
HEAD_GRID = (4, 2)

T = 128
F = 128
H = 4
SK = 64
GROUP = 4
DOCS_MOST = 8
LOW = -1e30
MESH = pl.DeviceIdType.MESH
F32 = jnp.float32
BF16 = jnp.bfloat16


def dot_nt(a, b):
    return lax.dot_general(a, b, (((1,), (1,)), ((), ())), preferred_element_type=F32)


def dot_nn(a, b):
    return jnp.dot(a, b, preferred_element_type=F32)


def sign_table(hashes):
    buckets = lax.broadcasted_iota(jnp.int32, (SK, hashes.shape[1]), 0)
    signs = (1 - 2 * (hashes[1:2, :] & 1)).astype(F32)
    return jnp.where(buckets == hashes[0:1, :], signs, 0.0).astype(BF16)


def rem(value, count):
    return lax.rem(value + count, count)


class Place:
    def __init__(self):
        self.planes, self.chips, self.cores = SEQ_GRID
        self.ys, self.halves = HEAD_GRID
        self.width = self.chips * self.cores
        seq = lax.axis_index("seq")
        head = lax.axis_index("head")
        self.seq, self.head = seq, head
        self.i = lax.rem(seq, self.width)
        self.z = seq // self.width
        self.c = lax.rem(self.i, self.cores)
        self.x = self.i // self.cores
        self.y = head // self.halves
        self.half = lax.rem(head, self.halves)

    def at(self, z=None, i=None, y=None, half=None):
        z = self.z if z is None else z
        i = self.i if i is None else i
        y = self.y if y is None else y
        half = self.half if half is None else half
        return (z * self.width + i, y * self.halves + half)


def remote(src, dst, send_sem, recv_sem, device):
    return pltpu.make_async_remote_copy(
        src_ref=src, dst_ref=dst, send_sem=send_sem, recv_sem=recv_sem, device_id=device, device_id_type=MESH
    )


def greet(devices):
    barrier = pltpu.get_barrier_semaphore()
    for device in devices:
        pl.semaphore_signal(barrier, inc=1, device_id=device, device_id_type=MESH)


def kernel(
    starts, targets, x_ref, q_ref, k_ref, v_ref, do_ref, xh_ref, qh_ref, kh_ref, vh_ref,
    out_ref,
    qall, kv, scores, wgrads, stat, kmt, stat_send, stat_recv, total, dq_acc, dkv_acc,
    dkv_send, dkv_recv, dq_send, dq_recv, iy, iz, grad_sum,
    products, near, plane_docs, far_send, far,
    q_recv, q_own, q_ring, q_sib, kv_send_sem, kv_recv_sem, st_send_sem, st_recv_sem,
    dkv_send_sem, dkv_recv_sem, dq_send_sem, dq_recv_sem, iy_send_sem, iy_recv_sem, iz_send_sem, iz_recv_sem,
    near_send_sem, near_recv_sem, plane_send_sem, plane_recv_sem, far_send_sem, far_recv_sem,
):
    me = Place()
    planes, chips, width = me.planes, me.chips, me.width
    x, c, z, i = me.x, me.c, me.z, me.i
    rows = 2 * T
    scale = 1.0 / math.sqrt(F)
    scale2 = scale * math.log2(math.e)

    ys, halves = me.ys, me.halves
    place_in_group = lax.rem(i, GROUP)
    group_first = i - place_in_group
    near_peers = []
    for o in range(1, GROUP * ys):
        near_peers.append((rem(place_in_group + o // ys, GROUP), rem(me.y + o % ys, ys)))
    far_peers = []
    for o in range(1, planes * halves):
        far_peers.append((rem(z + o // halves, planes), rem(me.half + o % halves, halves)))
    friends = [me.at(z=fz, half=half) for fz, half in far_peers]
    friends += [me.at(i=group_first + p, y=y) for n, (p, y) in enumerate(near_peers) if (n + 1) % ys]
    friends += [me.at(i=rem(i + o, width)) for o in range(1, width)]
    greet(friends)

    mine = pl.ds(pl.multiple_of(c * T, T), T)
    other = pl.ds(pl.multiple_of((1 - c) * T, T), T)
    for h in range(H):
        qall[x, 0, h, mine, :] = q_ref[:, h * F:(h + 1) * F]
        qall[x, 1, h, mine, :] = do_ref[:, h * F:(h + 1) * F]
    kv[z, 0] = k_ref[...]
    kv[z, 1] = v_ref[...]

    def piece(step, core, part):
        s = rem(x + step, chips)
        ref = qall.at[s, part, :, pl.ds(pl.multiple_of(core * T, T), T), :]
        return ref, q_recv.at[s, core, part]

    def send_piece(step, core, part, send_sem, target):
        ref, recv_sem = piece(step, core, part)
        return remote(ref, ref, send_sem, recv_sem, target)

    sibling = me.at(i=x * 2 + 1 - c)
    right = me.at(i=rem(x + 1, chips) * 2 + c)
    left = me.at(i=rem(x + chips - 1, chips) * 2 + c)
    own_copies = [
        send_piece(0, c, part, q_own.at[n, part], target)
        for n, target in enumerate((sibling, right, left)) for part in range(2)
    ]
    ring_copies = [
        send_piece(chips - 1, c, 0, q_ring.at[0], right),
        send_piece(1, c, 1, q_ring.at[1], left),
    ]
    sib_copies = {
        (step, part): send_piece(step, c, part, q_sib.at[step - 1, part], sibling)
        for step in (1, 2, 3) for part in range(2)
    }

    def wait_piece(step, core, part):
        ref, recv_sem = piece(step, core, part)
        remote(ref, ref, q_own.at[0, 0], recv_sem, sibling).wait_recv()

    def kv_copy(b, hops):
        return remote(
            kv.at[b], kv.at[b], kv_send_sem.at[b, hops - 1], kv_recv_sem.at[b], me.at(z=rem(z + hops, planes))
        )

    def relay_kv(b):
        @pl.when(z + 2 < planes)
        def _():
            kv_copy(b, 2).start()

        @pl.when(z + 1 < planes)
        def _():
            kv_copy(b, 1).start()

    input_part = dot_nt(sign_table(xh_ref[...]), x_ref[...])
    iy[me.y] = input_part.astype(BF16)
    query_table = sign_table(qh_ref[...])
    query_tables = jnp.concatenate([query_table[:, h * F:(h + 1) * F] for h in range(H)], axis=0)
    key_table = sign_table(kh_ref[...])
    value_table = sign_table(vh_ref[...])
    kmt[0] = dot_nt(query_tables, kv[z, 0]).astype(BF16)
    for s in range(chips):
        stat[s, 0:1, :] = jnp.full((1, H * rows), LOW, F32)
        stat[s, 1:3, :] = jnp.zeros((2, H * rows), F32)
    dq_acc[...] = jnp.zeros_like(dq_acc)
    dkv_acc[...] = jnp.zeros_like(dkv_acc)
    grad_sum[3 * SK:, :] = jnp.zeros((SK, T), F32)

    doc_count = starts.shape[0]
    group_tokens = GROUP * T
    tokens = lax.broadcasted_iota(jnp.int32, (1, T), 1)
    here = tokens + me.seq * T
    here_group = (me.seq // GROUP) * group_tokens
    slot_group = (z * (width // GROUP) + tokens // (2 * GROUP)) * group_tokens
    doc_of = jnp.zeros((1, T), jnp.int32)
    slot_first = jnp.zeros((1, T), jnp.int32)
    slot_past = jnp.zeros((1, T), jnp.int32)
    for d in range(doc_count):
        begins = starts[d]
        doc_of = doc_of + jnp.where(jnp.logical_and(begins <= here, begins > here_group), 1, 0)
        slot_first = slot_first + jnp.where(begins < slot_group, 1, 0)
        slot_past = slot_past + jnp.where(begins < slot_group + group_tokens, 1, 0)
    slot_doc = slot_first + lax.rem(tokens, 2 * GROUP)
    slot_doc = jnp.where(slot_doc < slot_past, slot_doc, -1)
    slot_row = jnp.full((1, T), -1, jnp.int32)
    for d in range(doc_count):
        slot_row = jnp.where(slot_doc == d, targets[d], slot_row)

    pl.semaphore_wait(pltpu.get_barrier_semaphore(), len(friends))

    relay_kv(z)
    for copy in own_copies:
        copy.start()

    iy_copies = [
        remote(iy.at[me.y], iy.at[me.y], iy_send_sem.at[o - 1], iy_recv_sem.at[me.y], me.at(y=rem(me.y + o, me.ys)))
        for o in range(1, me.ys)
    ]
    for copy in iy_copies:
        copy.start()
    iz_copy = remote(iz.at[me.half], iz.at[me.half], iz_send_sem.at[0], iz_recv_sem.at[me.half], me.at(half=1 - me.half))

    def input_over_y():
        for o in range(1, me.ys):
            y = rem(me.y + o, me.ys)
            remote(iy.at[y], iy.at[y], iy_send_sem.at[0], iy_recv_sem.at[y], me.at(y=y)).wait_recv()
        summed = iy[0].astype(F32)
        for y in range(1, me.ys):
            summed = summed + iy[y].astype(F32)
        iz[me.half] = summed.astype(BF16)
        if me.halves > 1:
            iz_copy.start()

    def first_unit(s, k, masked):
        b = z - k
        for h in range(H):
            cols = pl.ds(h * rows, rows)
            st = dot_nt(kv[b, 0], qall[s, 0, h]) * scale2
            if masked:
                key_place = lax.broadcasted_iota(jnp.int32, (T, rows), 0) + i * T
                query_place = lax.broadcasted_iota(jnp.int32, (T, rows), 1) + s * rows
                st = jnp.where(key_place <= query_place, st, LOW)
            dp = dot_nt(kv[b, 1], qall[s, 1, h])
            scores[s, k, :, cols] = st
            wgrads[s, k, :, cols] = dp
            old_top = stat[s, 0:1, cols]
            top = jnp.maximum(old_top, jnp.max(st, axis=0, keepdims=True))
            e = jnp.exp2(st - top)
            keep = jnp.exp2(old_top - top)
            stat[s, 0:1, cols] = top
            stat[s, 1:2, cols] = stat[s, 1:2, cols] * keep + jnp.sum(e, axis=0, keepdims=True)
            stat[s, 2:3, cols] = stat[s, 2:3, cols] * keep + jnp.sum(e * dp, axis=0, keepdims=True)

    def arrived_kv(t):
        b = z - t
        kv_copy(b, 1).wait_recv()
        kmt[t] = dot_nt(query_tables, kv[b, 0]).astype(BF16)

    def first_blocks(s, low, high):
        @pl.when(jnp.logical_and(low == 0, high > 0))
        def _():
            first_unit(s, 0, True)

        def over_blocks(k, carry):
            first_unit(s, k, False)
            return carry

        lax.fori_loop(jnp.maximum(low, 1), high, over_blocks, 0)

    def odd_arrivals(t):
        @pl.when(t <= z)
        def _():
            arrived_kv(t)

        @pl.when(t + 1 <= z)
        def _():
            arrived_kv(t + 1)
            relay_kv(z - t - 1)

    def first_step(t, carry):
        @pl.when(lax.rem(t, 2) == 1)
        def _():
            odd_arrivals(t)

        @pl.when(t == 0)
        def _():
            for part in range(2):
                wait_piece(0, 1 - c, part)

        @pl.when(t == 2)
        def _():
            for step in (chips - 1, 1):
                for part in range(2):
                    wait_piece(step, c, part)
                ring_copies[0 if step == chips - 1 else 1].start()
                for part in range(2):
                    sib_copies[(step, part)].start()

        @pl.when(t == 3)
        def _():
            for step in (chips - 1, 1):
                for part in range(2):
                    wait_piece(step, 1 - c, part)

        @pl.when(t == 4)
        def _():
            input_over_y()
            for part in range(2):
                wait_piece(2, c, part)
                sib_copies[(2, part)].start()

        def over_chips(r, carry):
            active = 3 * ((r + 1) // 2)
            low = jnp.where(t == active, 0, t)
            high = jnp.where(t >= active, jnp.minimum(t, z) + 1, 0)
            first_blocks(rem(x + r * (r + 1) // 2, chips), low, high)
            return carry

        return lax.fori_loop(0, chips - 1, over_chips, carry)

    lax.fori_loop(0, 6, first_step, 0)

    @pl.when(7 <= z)
    def _():
        arrived_kv(7)

    for part in range(2):
        wait_piece(2, 1 - c, part)

    pairs = chips // 2

    def stat_copies(g):
        return [
            remote(
                stat_send.at[g], stat_recv.at[g, i], st_send_sem.at[g, o - 1], st_recv_sem.at[g, i],
                me.at(i=rem(i + o, width)),
            )
            for o in range(1, width)
        ]

    def finish_chips(g, carry):
        def one_chip(n, carry):
            s = 2 * g + n
            first_blocks(s, jnp.where(s == rem(x + 2, chips), 0, 6), z + 1)
            return carry

        lax.fori_loop(0, 2, one_chip, 0)
        for n in range(2):
            stat_send[g, 3 * n:3 * n + 3, :] = stat[2 * g + n, 0:3, :]
        for copy in stat_copies(g):
            copy.start()
        stat_recv[g, i] = stat_send[g]
        return carry

    lax.fori_loop(0, pairs, finish_chips, 0)

    def add_statistics(g):
        for o in range(1, width):
            p = rem(i + o, width)
            remote(
                stat_send.at[g], stat_recv.at[g, p], st_send_sem.at[g, 0], st_recv_sem.at[g, p], me.at(i=p)
            ).wait_recv()
        for n in range(2):
            first = 3 * n
            top = stat_recv[g, 0, first:first + 1, :]
            for p in range(1, width):
                top = jnp.maximum(top, stat_recv[g, p, first:first + 1, :])
            weight_sum = jnp.zeros_like(top)
            delta_sum = jnp.zeros_like(top)
            for p in range(width):
                factor = jnp.exp2(stat_recv[g, p, first:first + 1, :] - top)
                weight_sum = weight_sum + stat_recv[g, p, first + 1:first + 2, :] * factor
                delta_sum = delta_sum + stat_recv[g, p, first + 2:first + 3, :] * factor
            total[2 * g + n, 0:1, :] = top + jnp.log2(weight_sum)
            total[2 * g + n, 1:2, :] = delta_sum / weight_sum

    def second_unit(s, k):
        lows, grads = [], []
        for h in range(H):
            cols = pl.ds(h * rows, rows)
            p = jnp.exp2(scores[s, k, :, cols] - total[s, 0:1, cols])
            g = p * (wgrads[s, k, :, cols] - total[s, 1:2, cols])
            lows.append(p.astype(BF16))
            g = g.astype(BF16)
            grads.append(g)
            dq_acc[s] += dot_nn(kmt[k, h * SK:(h + 1) * SK, :], g)
        low = jnp.concatenate(lows, axis=1)
        grad = jnp.concatenate(grads, axis=1)
        dkv_acc[k, 0] += dot_nn(grad, qall[s, 0].reshape(H * rows, F))
        dkv_acc[k, 1] += dot_nn(low, qall[s, 1].reshape(H * rows, F))

    def dkv_copy(k, b):
        return remote(dkv_send.at[k], dkv_recv.at[z], dkv_send_sem.at[k], dkv_recv_sem.at[z], me.at(z=b))

    def send_dq(g):
        for s in (2 * g, 2 * g + 1):
            for core in range(2):
                dq_send[s * 2 + core] = (dq_acc[s, :, core * T:(core + 1) * T] * scale).astype(BF16)
        for n in range(GROUP):
            p = GROUP * g + n

            @pl.when(p != i)
            def _():
                dq_copy(p).start()

    def dq_copy(p):
        return remote(dq_send.at[p], dq_recv.at[i], dq_send_sem.at[p], dq_recv_sem.at[i], me.at(i=p))

    for g in range(pairs - 1):
        add_statistics(g)

        def half_blocks(k, carry):
            def over_chips(n, carry):
                second_unit(2 * g + n, k)
                return carry

            return lax.fori_loop(0, 2, over_chips, carry)

        lax.fori_loop(0, z + 1, half_blocks, 0)
        send_dq(g)
    add_statistics(pairs - 1)

    def second_step(n, carry):
        k = z - n

        def over_chips(m, carry):
            second_unit(chips - 2 + m, k)
            return carry

        lax.fori_loop(0, 2, over_chips, 0)
        dkv_send[k, 0:SK, :] = dot_nt(key_table, (dkv_acc[k, 0] * scale).astype(BF16)).astype(BF16)
        dkv_send[k, SK:, :] = dot_nt(value_table, dkv_acc[k, 1].astype(BF16)).astype(BF16)

        @pl.when(k > 0)
        def _():
            dkv_copy(k, n).start()

        return carry

    lax.fori_loop(0, z + 1, second_step, 0)
    send_dq(pairs - 1)

    if me.halves > 1:
        away = 1 - me.half
        remote(iz.at[away], iz.at[away], iz_send_sem.at[0], iz_recv_sem.at[away], me.at(half=away)).wait_recv()
    summed = iz[0].astype(F32)
    for half in range(1, me.halves):
        summed = summed + iz[half].astype(F32)
    input_sketch = summed * math.sqrt(SK / (x_ref.shape[1] * ys * halves))

    heads = me.ys * me.halves
    kv_factor = math.sqrt(SK / (F * heads))
    grad_sum[SK:3 * SK, :] = dkv_send[0].astype(F32) * kv_factor

    def add_kv(b, carry):
        remote(dkv_send.at[0], dkv_recv.at[b], dkv_send_sem.at[0], dkv_recv_sem.at[b], me.at(z=rem(z + 1, planes))).wait_recv()
        grad_sum[SK:3 * SK, :] += dkv_recv[b].astype(F32) * kv_factor
        return carry

    dq_recv[i] = dq_send[i]
    lax.fori_loop(z + 1, planes, add_kv, 0)
    for o in range(1, width):
        p = rem(i + o, width)
        remote(dq_send.at[p], dq_recv.at[p], dq_send_sem.at[0], dq_recv_sem.at[p], me.at(i=p)).wait_recv()
    query_sum = dq_recv[0].astype(F32)
    for p in range(1, width):
        query_sum = query_sum + dq_recv[p].astype(F32)
    grad_sum[0:SK, :] = query_sum * math.sqrt(SK / (H * F * heads))

    band = SK // ys
    masked = jnp.concatenate([jnp.where(doc_of == e, input_sketch, 0.0) for e in range(DOCS_MOST)], axis=0)
    grads = grad_sum[...]
    masked_high = masked.astype(BF16)
    masked_low = (masked - masked_high.astype(F32)).astype(BF16)
    grads_high = grads.astype(BF16)
    grads_low = (grads - grads_high.astype(F32)).astype(BF16)
    product = dot_nt(masked_high, grads_high) + (dot_nt(masked_high, grads_low) + dot_nt(masked_low, grads_high))
    products[...] = product.reshape(DOCS_MOST, SK, 4 * SK).astype(BF16)

    def part(p, y):
        return products.at[pl.ds(p * 2, 2), pl.ds(pl.multiple_of(y * band, band), band), :]

    my_slot = place_in_group * ys + me.y
    near_copies = [
        remote(part(p, y), near.at[my_slot], near_send_sem.at[n], near_recv_sem.at[my_slot], me.at(i=group_first + p, y=y))
        for n, (p, y) in enumerate(near_peers)
    ]
    for copy in near_copies:
        copy.start()
    summed = part(place_in_group, me.y)[...].astype(F32)
    for p, y in near_peers:
        slot = p * ys + y
        remote(near.at[slot], near.at[slot], near_send_sem.at[0], near_recv_sem.at[slot], me.at(i=group_first + p, y=y)).wait_recv()
        summed = summed + near[slot].astype(F32)
    plane_docs[i] = summed.astype(BF16)

    plane_copies = [
        remote(plane_docs.at[i], plane_docs.at[i], plane_send_sem.at[o - 1], plane_recv_sem.at[i], me.at(i=rem(i + o, width)))
        for o in range(1, width)
    ]
    for copy in plane_copies:
        copy.start()
    for o in range(1, width):
        p = rem(i + o, width)
        remote(plane_docs.at[p], plane_docs.at[p], plane_send_sem.at[0], plane_recv_sem.at[p], me.at(i=p)).wait_recv()

    def gather_row(fz, carry):
        row = fz * width + i
        found = jnp.zeros((band, 4 * SK), F32)
        for j in range(width):
            for e in range(2):
                chosen = jnp.broadcast_to(slot_row[:, 2 * j + e:2 * j + e + 1], (band, 4 * SK)) == row
                found = found + jnp.where(chosen, plane_docs[j, e].astype(F32), 0.0)
        own = band // halves
        for half in range(halves):
            rows_half = found[half * own:(half + 1) * own, :]
            both = jnp.concatenate([rows_half[:, 0:2 * SK], rows_half[:, 2 * SK:]], axis=0)
            far_send[fz * halves + half] = both.astype(BF16)
        return carry

    lax.fori_loop(0, planes, gather_row, 0)
    my_line = z * halves + me.half
    far_copies = [
        remote(far_send.at[fz * halves + half], far.at[my_line], far_send_sem.at[n], far_recv_sem.at[my_line], me.at(z=fz, half=half))
        for n, (fz, half) in enumerate(far_peers)
    ]
    for copy in far_copies:
        copy.start()
    result = far_send[my_line].astype(F32)
    for fz, half in far_peers:
        slot = fz * halves + half
        remote(far.at[slot], far.at[slot], far_send_sem.at[0], far_recv_sem.at[slot], me.at(z=fz, half=half)).wait_recv()
        result = result + far[slot].astype(F32)
    own = band // halves
    out_ref[...] = jnp.concatenate([result[0:own], result[own:]], axis=1)

    for copy in own_copies + ring_copies + list(sib_copies.values()) + iy_copies + near_copies + plane_copies + far_copies:
        copy.wait_send()
    if me.halves > 1:
        iz_copy.wait_send()

    for g in range(pairs):
        for copy in stat_copies(g):
            copy.wait_send()
    for p in range(width):
        @pl.when(p != i)
        def _():
            dq_copy(p).wait_send()

    def left_kv(n, carry):
        b = z - 2 * n

        @pl.when(z + 2 < planes)
        def _():
            kv_copy(b, 2).wait_send()

        @pl.when(z + 1 < planes)
        def _():
            kv_copy(b, 1).wait_send()

        return carry

    lax.fori_loop(0, z // 2 + 1, left_kv, 0)

    def left_dkv(k, carry):
        dkv_copy(k, z - k).wait_send()
        return carry

    lax.fori_loop(1, z + 1, left_dkv, 0)


def sketches_of(
    doc_starts, doc_rows, layer_input, queries, key_states, value_states, out_grad,
    input_hash, query_hash, key_hash, value_hash,
):
    planes, chips, cores = SEQ_GRID
    ys, halves = HEAD_GRID
    width = chips * cores
    rows = 2 * T
    line = planes * halves
    band = SK // ys
    pairs = chips // 2
    dma = pltpu.SemaphoreType.DMA
    vmem = pltpu.VMEM
    return pl.pallas_call(
        kernel,
        out_shape=jax.ShapeDtypeStruct((band // halves, 4 * SK), F32),
        in_specs=[pl.BlockSpec(memory_space=pltpu.SMEM)] * 2 + [pl.BlockSpec(memory_space=pltpu.VMEM)] * 9,
        out_specs=pl.BlockSpec(memory_space=pltpu.VMEM),
        scratch_shapes=[
            vmem((chips, 2, H, rows, F), BF16),
            vmem((planes, 2, T, F), BF16),
            vmem((chips, planes, T, H * rows), F32),
            vmem((chips, planes, T, H * rows), F32),
            vmem((chips, 8, H * rows), F32),
            vmem((planes, H * SK, T), BF16),
            vmem((pairs, 8, H * rows), F32),
            vmem((pairs, width, 8, H * rows), F32),
            vmem((chips, 8, H * rows), F32),
            vmem((chips, SK, rows), F32),
            vmem((planes, 2, T, F), F32),
            vmem((planes, 2 * SK, T), BF16),
            vmem((planes, 2 * SK, T), BF16),
            vmem((width, SK, T), BF16),
            vmem((width, SK, T), BF16),
            vmem((ys, SK, T), BF16),
            vmem((halves, SK, T), BF16),
            vmem((4 * SK, T), F32),
            vmem((DOCS_MOST, SK, 4 * SK), BF16),
            vmem((GROUP * ys, 2, band, 4 * SK), BF16),
            vmem((width, 2, band, 4 * SK), BF16),
            vmem((line, 2 * band // halves, 2 * SK), BF16),
            vmem((line, 2 * band // halves, 2 * SK), BF16),
            dma((chips, 2, 2)), dma((3, 2)), dma((2,)), dma((3, 2)),
            dma((planes, 2)), dma((planes,)),
            dma((pairs, width)), dma((pairs, width)),
            dma((planes,)), dma((planes,)),
            dma((width,)), dma((width,)),
            dma((ys,)), dma((ys,)), dma((halves,)), dma((halves,)),
            dma((GROUP * ys,)), dma((GROUP * ys,)),
            dma((width,)), dma((width,)),
            dma((line,)), dma((line,)),
        ],
        compiler_params=pltpu.CompilerParams(
            collective_id=0, has_side_effects=True, vmem_limit_bytes=56 * 1024 * 1024
        ),
        name="sketches",
    )(
        doc_starts, doc_rows, layer_input, queries, key_states, value_states, out_grad,
        input_hash, query_hash, key_hash, value_hash,
    )


def on_device(
    layer_input, queries, key_states, value_states, out_grad,
    input_hash, query_hash, key_hash, value_hash, doc_starts, doc_rows,
):
    result = sketches_of(
        doc_starts, doc_rows, layer_input, queries, key_states, value_states, out_grad,
        input_hash, query_hash, key_hash, value_hash,
    )
    bands = result.shape[0]
    return result[:, :3 * SK].reshape(bands, 3, SK).transpose(1, 0, 2).reshape(1, 3, bands * SK)


def solution(mesh):
    return jax.shard_map(
        on_device,
        mesh=mesh,
        in_specs=(
            P("seq", "head"), P("seq", "head"), P("seq", "head"), P("seq", "head"), P("seq", "head"),
            P(None, "head"), P(None, "head"), P(None, "head"), P(None, "head"),
            P(), P(),
        ),
        out_specs=P("seq", None, "head"),
        check_vma=False,
    )
```

time: 97.7 us -> 87.6 us (0.90)
  Pallas kernels: 96.1 us -> 85.9 us
    pallas_call x2 -> x1, Pallas kernels: 96.1 us -> 85.9 us  [sketches_of(): pl.pallas_call(kernel, out_shape=jax.ShapeDtypeStruct((band // halves, 4...]
where the time goes in v2:
time: 87.6 us; the launch traced here: 87.4 us
  Pallas kernels  85.9 us (98%)
  local copies, waits for them, and re-layouts  1.45 us (2%)
    pallas_call x1, Pallas kernels, sketches_of(): pl.pallas_call(kernel, out_shape=jax.ShapeDtypeStruct((band // halves, 4...  85.9 us

profile of v2, /device:TPU:1, one launch (start us, length us, event | category | flops | bytes accessed | tf_op | source)
XLA Modules:
  0.0 87.4 jit_solution(9792158412350841208)
XLA Ops:
  0.0 85.9 %sketches.1 = f32[8,256]{1,0:T(8,128)} custom-call(s32[64]{0:T(128)} %starts.1, s32[64]{0:T(128)} %targets.1, bf16[128,1024]{1,0:T(8,128)(2,1)} %x_ref.1, bf16[128,512]{1,0:T(8,128)(2,1)} %q_ref.1, bf16[128,128]{1,0:T(8,128)(2,1)} %k_ref.1, bf16[128,128]{1,0:T(8,128)(2,1)} %v_ref.1, bf16[128,512]{1,0:T(8,128)(2,1)} %do_ref.1, s32[2,1024]{1,0:T(2,128)} %xh_ref.1, ...), custom_call_target="tpu_custom_call" | custom-call | tf_op jit(solution)/shard_map/sketches/pallas_call | solution.py:571
  85.9 0.8 reshape.6
  86.7 0.7 reshape.8
  (1 shorter events, 0.0 us)

commit v3 on v2

--- a/solution.py
+++ b/solution.py
@@ -82,7 +82,7 @@
     qall, kv, scores, wgrads, stat, kmt, stat_send, stat_recv, total, dq_acc, dkv_acc,
     dkv_send, dkv_recv, dq_send, dq_recv, iy, iz, grad_sum,
     products, near, plane_docs, far_send, far,
-    q_recv, q_own, q_ring, q_sib, kv_send_sem, kv_recv_sem, st_send_sem, st_recv_sem,
+    inputs, input_sem, hello, q_recv, q_own, q_ring, q_sib, kv_send_sem, kv_recv_sem, st_send_sem, st_recv_sem,
     dkv_send_sem, dkv_recv_sem, dq_send_sem, dq_recv_sem, iy_send_sem, iy_recv_sem, iz_send_sem, iz_recv_sem,
     near_send_sem, near_recv_sem, plane_send_sem, plane_recv_sem, far_send_sem, far_recv_sem,
 ):
@@ -102,18 +102,41 @@
     far_peers = []
     for o in range(1, planes * halves):
         far_peers.append((rem(z + o // halves, planes), rem(me.half + o % halves, halves)))
-    friends = [me.at(z=fz, half=half) for fz, half in far_peers]
+    line = planes * halves
+
+    def along(steps):
+        to = rem(me.half * planes + z + steps, line)
+        return me.at(z=lax.rem(to, planes), half=to // planes)
+
+    friends = [along(o) for o in sorted({o % line for o in (1, 2, -1, -2)} - {0})]
+    hellos = 3 if line > 5 else 0
+
+    def pass_hello(n):
+        for steps in (2, -2):
+            pl.semaphore_signal(hello.at[n], inc=1, device_id=along(steps), device_id_type=MESH)
+
+    def hear_hello(n):
+        pl.semaphore_wait(hello.at[n], 2)
+
     friends += [me.at(i=group_first + p, y=y) for n, (p, y) in enumerate(near_peers) if (n + 1) % ys]
     friends += [me.at(i=rem(i + o, width)) for o in range(1, width)]
     greet(friends)
 
     mine = pl.ds(pl.multiple_of(c * T, T), T)
-    other = pl.ds(pl.multiple_of((1 - c) * T, T), T)
-    for h in range(H):
-        qall[x, 0, h, mine, :] = q_ref[:, h * F:(h + 1) * F]
-        qall[x, 1, h, mine, :] = do_ref[:, h * F:(h + 1) * F]
-    kv[z, 0] = k_ref[...]
-    kv[z, 1] = v_ref[...]
+    loads = [pltpu.make_async_copy(k_ref, kv.at[z, 0], input_sem.at[0]), pltpu.make_async_copy(v_ref, kv.at[z, 1], input_sem.at[1])]
+    for part, ref in enumerate((q_ref, do_ref)):
+        for h in range(H):
+            loads.append(
+                pltpu.make_async_copy(
+                    ref.at[:, pl.ds(h * F, F)], qall.at[x, part, h, mine, :], input_sem.at[2 + part * H + h]
+                )
+            )
+    load_input = pltpu.make_async_copy(x_ref, inputs, input_sem.at[2 + 2 * H])
+    for load in loads:
+        load.start()
+    load_input.start()
+    for load in loads:
+        load.wait()
 
     def piece(step, core, part):
         s = rem(x + step, chips)
@@ -144,21 +167,33 @@
         ref, recv_sem = piece(step, core, part)
         remote(ref, ref, q_own.at[0, 0], recv_sem, sibling).wait_recv()
 
-    def kv_copy(b, hops):
+    def kv_copy(b, hops, part):
         return remote(
-            kv.at[b], kv.at[b], kv_send_sem.at[b, hops - 1], kv_recv_sem.at[b], me.at(z=rem(z + hops, planes))
+            kv.at[b, part], kv.at[b, part], kv_send_sem.at[b, hops - 1, part], kv_recv_sem.at[b, part],
+            me.at(z=rem(z + hops, planes)),
         )
 
-    def relay_kv(b):
+    def relay_kv(b, part):
         @pl.when(z + 2 < planes)
         def _():
-            kv_copy(b, 2).start()
+            kv_copy(b, 2, part).start()
 
         @pl.when(z + 1 < planes)
         def _():
-            kv_copy(b, 1).start()
-
-    input_part = dot_nt(sign_table(xh_ref[...]), x_ref[...])
+            kv_copy(b, 1, part).start()
+
+    pl.semaphore_wait(pltpu.get_barrier_semaphore(), len(friends))
+
+    for part in range(2):
+        relay_kv(z, part)
+    for target, part in ((1, 0), (2, 1), (0, 0), (0, 1), (1, 1), (2, 0)):
+        own_copies[2 * target + part].start()
+
+    if hellos:
+        pass_hello(0)
+    load_input.wait()
+
+    input_part = dot_nt(sign_table(xh_ref[...]), inputs[...])
     iy[me.y] = input_part.astype(BF16)
     query_table = sign_table(qh_ref[...])
     query_tables = jnp.concatenate([query_table[:, h * F:(h + 1) * F] for h in range(H)], axis=0)
@@ -192,12 +227,6 @@
     for d in range(doc_count):
         slot_row = jnp.where(slot_doc == d, targets[d], slot_row)
 
-    pl.semaphore_wait(pltpu.get_barrier_semaphore(), len(friends))
-
-    relay_kv(z)
-    for copy in own_copies:
-        copy.start()
-
     iy_copies = [
         remote(iy.at[me.y], iy.at[me.y], iy_send_sem.at[o - 1], iy_recv_sem.at[me.y], me.at(y=rem(me.y + o, me.ys)))
         for o in range(1, me.ys)
@@ -214,8 +243,6 @@
         for y in range(1, me.ys):
             summed = summed + iy[y].astype(F32)
         iz[me.half] = summed.astype(BF16)
-        if me.halves > 1:
-            iz_copy.start()
 
     def first_unit(s, k, masked):
         b = z - k
@@ -238,9 +265,11 @@
             stat[s, 2:3, cols] = stat[s, 2:3, cols] * keep + jnp.sum(e * dp, axis=0, keepdims=True)
 
     def arrived_kv(t):
-        b = z - t
-        kv_copy(b, 1).wait_recv()
-        kmt[t] = dot_nt(query_tables, kv[b, 0]).astype(BF16)
+        for part in range(2):
+            kv_copy(z - t, 1, part).wait_recv()
+
+    def sketch_keys(t):
+        kmt[t] = dot_nt(query_tables, kv[z - t, 0]).astype(BF16)
 
     def first_blocks(s, low, high):
         @pl.when(jnp.logical_and(low == 0, high > 0))
@@ -254,14 +283,20 @@
         lax.fori_loop(jnp.maximum(low, 1), high, over_blocks, 0)
 
     def odd_arrivals(t):
+        @pl.when(t + 1 <= z)
+        def _():
+            for part in range(2):
+                kv_copy(z - t - 1, 1, part).wait_recv()
+                relay_kv(z - t - 1, part)
+
         @pl.when(t <= z)
         def _():
             arrived_kv(t)
+            sketch_keys(t)
 
         @pl.when(t + 1 <= z)
         def _():
-            arrived_kv(t + 1)
-            relay_kv(z - t - 1)
+            sketch_keys(t + 1)
 
     def first_step(t, carry):
         @pl.when(lax.rem(t, 2) == 1)
@@ -273,14 +308,20 @@
             for part in range(2):
                 wait_piece(0, 1 - c, part)
 
+        if hellos:
+            for n in (1, 2):
+                @pl.when(t == 2 * n)
+                def _():
+                    hear_hello(n - 1)
+                    pass_hello(n)
+
         @pl.when(t == 2)
         def _():
-            for step in (chips - 1, 1):
-                for part in range(2):
-                    wait_piece(step, c, part)
-                ring_copies[0 if step == chips - 1 else 1].start()
-                for part in range(2):
-                    sib_copies[(step, part)].start()
+            for n, (step, part) in enumerate(((chips - 1, 0), (1, 1), (chips - 1, 1), (1, 0))):
+                wait_piece(step, c, part)
+                if n < 2:
+                    ring_copies[n].start()
+                sib_copies[(step, part)].start()
 
         @pl.when(t == 3)
         def _():
@@ -309,6 +350,7 @@
     @pl.when(7 <= z)
     def _():
         arrived_kv(7)
+        sketch_keys(7)
 
     for part in range(2):
         wait_piece(2, 1 - c, part)
@@ -339,6 +381,10 @@
         return carry
 
     lax.fori_loop(0, pairs, finish_chips, 0)
+    if hellos:
+        hear_hello(2)
+    if me.halves > 1:
+        iz_copy.start()
 
     def add_statistics(g):
         for o in range(1, width):
@@ -392,28 +438,31 @@
     def dq_copy(p):
         return remote(dq_send.at[p], dq_recv.at[i], dq_send_sem.at[p], dq_recv_sem.at[i], me.at(i=p))
 
-    for g in range(pairs - 1):
-        add_statistics(g)
-
-        def half_blocks(k, carry):
-            def over_chips(n, carry):
-                second_unit(2 * g + n, k)
-                return carry
-
-            return lax.fori_loop(0, 2, over_chips, carry)
-
-        lax.fori_loop(0, z + 1, half_blocks, 0)
-        send_dq(g)
-    add_statistics(pairs - 1)
+    near_blocks = (z + 2) // 2
+    add_statistics(0)
+
+    def half_blocks(k, carry):
+        def over_chips(s, carry):
+            second_unit(s, k)
+            return carry
+
+        return lax.fori_loop(0, 2, over_chips, carry)
+
+    lax.fori_loop(0, near_blocks, half_blocks, 0)
+    add_statistics(1)
 
     def second_step(n, carry):
         k = z - n
 
-        def over_chips(m, carry):
-            second_unit(chips - 2 + m, k)
+        @pl.when(k == near_blocks - 1)
+        def _():
+            send_dq(0)
+
+        def over_chips(s, carry):
+            second_unit(s, k)
             return carry
 
-        lax.fori_loop(0, 2, over_chips, 0)
+        lax.fori_loop(jnp.where(k < near_blocks, 2, 0), chips, over_chips, 0)
         dkv_send[k, 0:SK, :] = dot_nt(key_table, (dkv_acc[k, 0] * scale).astype(BF16)).astype(BF16)
         dkv_send[k, SK:, :] = dot_nt(value_table, dkv_acc[k, 1].astype(BF16)).astype(BF16)
 
@@ -424,7 +473,7 @@
         return carry
 
     lax.fori_loop(0, z + 1, second_step, 0)
-    send_dq(pairs - 1)
+    send_dq(1)
 
     if me.halves > 1:
         away = 1 - me.half
@@ -518,7 +567,14 @@
         remote(far.at[slot], far.at[slot], far_send_sem.at[0], far_recv_sem.at[slot], me.at(z=fz, half=half)).wait_recv()
         result = result + far[slot].astype(F32)
     own = band // halves
-    out_ref[...] = jnp.concatenate([result[0:own], result[own:]], axis=1)
+    query_key, value_only = result[0:own], result[own:]
+    key_query, moved_value = pltpu.roll(query_key, SK, 1), pltpu.roll(value_only, SK, 1)
+    first_half = lax.broadcasted_iota(jnp.int32, (1, 2 * SK), 1) < SK
+    for p, (even, odd) in enumerate(((query_key, key_query), (key_query, query_key), (value_only, moved_value))):
+        for pair in range(own // 2):
+            out_ref[0, p:p + 1, pair * 2 * SK:(pair + 1) * 2 * SK] = jnp.where(
+                first_half, even[2 * pair:2 * pair + 1], odd[2 * pair + 1:2 * pair + 2]
+            )
 
     for copy in own_copies + ring_copies + list(sib_copies.values()) + iy_copies + near_copies + plane_copies + far_copies:
         copy.wait_send()
@@ -536,13 +592,14 @@
     def left_kv(n, carry):
         b = z - 2 * n
 
-        @pl.when(z + 2 < planes)
-        def _():
-            kv_copy(b, 2).wait_send()
-
-        @pl.when(z + 1 < planes)
-        def _():
-            kv_copy(b, 1).wait_send()
+        for part in range(2):
+            @pl.when(z + 2 < planes)
+            def _():
+                kv_copy(b, 2, part).wait_send()
+
+            @pl.when(z + 1 < planes)
+            def _():
+                kv_copy(b, 1, part).wait_send()
 
         return carry
 
@@ -570,8 +627,9 @@
     vmem = pltpu.VMEM
     return pl.pallas_call(
         kernel,
-        out_shape=jax.ShapeDtypeStruct((band // halves, 4 * SK), F32),
-        in_specs=[pl.BlockSpec(memory_space=pltpu.SMEM)] * 2 + [pl.BlockSpec(memory_space=pltpu.VMEM)] * 9,
+        out_shape=jax.ShapeDtypeStruct((1, 3, band // halves * SK), F32),
+        in_specs=[pl.BlockSpec(memory_space=pltpu.SMEM)] * 2 + [pl.BlockSpec(memory_space=pl.ANY)] * 5
+        + [pl.BlockSpec(memory_space=pltpu.VMEM)] * 4,
         out_specs=pl.BlockSpec(memory_space=pltpu.VMEM),
         scratch_shapes=[
             vmem((chips, 2, H, rows, F), BF16),
@@ -597,8 +655,10 @@
             vmem((width, 2, band, 4 * SK), BF16),
             vmem((line, 2 * band // halves, 2 * SK), BF16),
             vmem((line, 2 * band // halves, 2 * SK), BF16),
+            vmem(layer_input.shape, BF16),
+            dma((2 + 2 * H + 1,)), pltpu.SemaphoreType.REGULAR((3,)),
             dma((chips, 2, 2)), dma((3, 2)), dma((2,)), dma((3, 2)),
-            dma((planes, 2)), dma((planes,)),
+            dma((planes, 2, 2)), dma((planes, 2)),
             dma((pairs, width)), dma((pairs, width)),
             dma((planes,)), dma((planes,)),
             dma((width,)), dma((width,)),
@@ -621,12 +681,10 @@
     layer_input, queries, key_states, value_states, out_grad,
     input_hash, query_hash, key_hash, value_hash, doc_starts, doc_rows,
 ):
-    result = sketches_of(
+    return sketches_of(
         doc_starts, doc_rows, layer_input, queries, key_states, value_states, out_grad,
         input_hash, query_hash, key_hash, value_hash,
     )
-    bands = result.shape[0]
-    return result[:, :3 * SK].reshape(bands, 3, SK).transpose(1, 0, 2).reshape(1, 3, bands * SK)
 
 
 def solution(mesh):

time: 87.6 us -> 80 us (0.913)
  Pallas kernels: 85.9 us -> 78.4 us
    pallas_call x1, Pallas kernels: 85.9 us -> 78.4 us  [sketches_of(): pl.pallas_call(kernel, out_shape=jax.ShapeDtypeStruct((1, 3, band // halv...]
    reshape x2 -> x0, local copies, waits for them, and re-layouts: 1.45 us -> none  [on_device(): result[:, :3 * SK].reshape(bands, 3, SK).transpose(1, 0, 2)]
    pallas_call x0 -> x1, local copies, waits for them, and re-layouts: none -> 1.3 us  [sketches_of(): pl.pallas_call(kernel, out_shape=jax.ShapeDtypeStruct((1, 3, band // halv...]
where the time goes in v3:
time: 80 us; the launch traced here: 79.8 us
  Pallas kernels  78.4 us (98%)
  local copies, waits for them, and re-layouts  1.3 us (2%)
    pallas_call x1, Pallas kernels, sketches_of(): pl.pallas_call(kernel, out_shape=jax.ShapeDtypeStruct((1, 3, band // halv...  78.4 us

profile of v3, /device:TPU:1, one launch (start us, length us, event | category | flops | bytes accessed | tf_op | source)
XLA Modules:
  0.0 79.8 jit_solution(7918079254553927246)
XLA Ops:
  0.0 78.4 %sketches.1 = f32[1,3,512]{2,1,0:T(4,128)} custom-call(s32[64]{0:T(128)} %starts.1, s32[64]{0:T(128)} %targets.1, bf16[128,1024]{1,0:T(8,128)(2,1)} %x_ref.1, bf16[128,512]{1,0:T(8,128)(2,1)} %q_ref.1, bf16[128,128]{1,0:T(8,128)(2,1)} %k_ref.1, bf16[128,128]{1,0:T(8,128)(2,1)} %v_ref.1, bf16[128,512]{1,0:T(8,128)(2,1)} %do_ref.1, s32[2,1024]{1,0:T(2,128)} %xh_ref.1, ...), custom_call_target="tpu_custom_call" | custom-call | tf_op jit(solution)/shard_map/sketches/pallas_call | solution.py:628
  78.5 1.3 %copy.12 = f32[1,3,512]{2,0,1:T(1,128)} copy(f32[1,3,512]{2,1,0:T(4,128)} %sketches.1) | data formatting | bytes 12288 | tf_op jit(solution)/shard_map/sketches/pallas_call | solution.py:628

commit v4 on v3

--- a/solution.py
+++ b/solution.py
@@ -77,14 +77,14 @@
 
 
 def kernel(
-    starts, targets, x_ref, q_ref, k_ref, v_ref, do_ref, xh_ref, qh_ref, kh_ref, vh_ref,
+    starts_ref, targets_ref, x_ref, q_ref, k_ref, v_ref, do_ref, xh_ref, qh_ref, kh_ref, vh_ref,
     out_ref,
     qall, kv, scores, wgrads, stat, kmt, stat_send, stat_recv, total, dq_acc, dkv_acc,
     dkv_send, dkv_recv, dq_send, dq_recv, iy, iz, grad_sum,
     products, near, plane_docs, far_send, far,
-    inputs, input_sem, hello, q_recv, q_own, q_ring, q_sib, kv_send_sem, kv_recv_sem, st_send_sem, st_recv_sem,
+    inputs, starts, targets, input_hash, query_hash, key_hash, value_hash, input_sem, hello, q_recv, q_own, q_ring, q_sib, kv_send_sem, kv_recv_sem, pool, st_recv_sem,
     dkv_send_sem, dkv_recv_sem, dq_send_sem, dq_recv_sem, iy_send_sem, iy_recv_sem, iz_send_sem, iz_recv_sem,
-    near_send_sem, near_recv_sem, plane_send_sem, plane_recv_sem, far_send_sem, far_recv_sem,
+    near_recv_sem, plane_recv_sem, far_recv_sem,
 ):
     me = Place()
     planes, chips, width = me.planes, me.chips, me.width
@@ -118,7 +118,7 @@
     def hear_hello(n):
         pl.semaphore_wait(hello.at[n], 2)
 
-    friends += [me.at(i=group_first + p, y=y) for n, (p, y) in enumerate(near_peers) if (n + 1) % ys]
+    friends += [me.at(y=rem(me.y + o, ys)) for o in range(1, ys)]
     friends += [me.at(i=rem(i + o, width)) for o in range(1, width)]
     greet(friends)
 
@@ -131,10 +131,15 @@
                     ref.at[:, pl.ds(h * F, F)], qall.at[x, part, h, mine, :], input_sem.at[2 + part * H + h]
                 )
             )
-    load_input = pltpu.make_async_copy(x_ref, inputs, input_sem.at[2 + 2 * H])
-    for load in loads:
+    later = (
+        (x_ref, inputs), (xh_ref, input_hash), (qh_ref, query_hash), (kh_ref, key_hash), (vh_ref, value_hash),
+        (starts_ref, starts), (targets_ref, targets),
+    )
+    later_loads = [
+        pltpu.make_async_copy(ref, place, input_sem.at[2 + 2 * H + n]) for n, (ref, place) in enumerate(later)
+    ]
+    for load in loads + later_loads:
         load.start()
-    load_input.start()
     for load in loads:
         load.wait()
 
@@ -169,7 +174,7 @@
 
     def kv_copy(b, hops, part):
         return remote(
-            kv.at[b, part], kv.at[b, part], kv_send_sem.at[b, hops - 1, part], kv_recv_sem.at[b, part],
+            kv.at[b, part], kv.at[b, part], kv_send_sem.at[b // 2, hops - 1, part], kv_recv_sem.at[b, part],
             me.at(z=rem(z + hops, planes)),
         )
 
@@ -191,15 +196,15 @@
 
     if hellos:
         pass_hello(0)
-    load_input.wait()
-
-    input_part = dot_nt(sign_table(xh_ref[...]), inputs[...])
+    for load in later_loads:
+        load.wait()
+
+    input_part = dot_nt(sign_table(input_hash[...]), inputs[...])
     iy[me.y] = input_part.astype(BF16)
-    query_table = sign_table(qh_ref[...])
+    query_table = sign_table(query_hash[...])
     query_tables = jnp.concatenate([query_table[:, h * F:(h + 1) * F] for h in range(H)], axis=0)
-    key_table = sign_table(kh_ref[...])
-    value_table = sign_table(vh_ref[...])
-    kmt[0] = dot_nt(query_tables, kv[z, 0]).astype(BF16)
+    key_table = sign_table(key_hash[...])
+    value_table = sign_table(value_hash[...])
     for s in range(chips):
         stat[s, 0:1, :] = jnp.full((1, H * rows), LOW, F32)
         stat[s, 1:3, :] = jnp.zeros((2, H * rows), F32)
@@ -244,18 +249,25 @@
             summed = summed + iy[y].astype(F32)
         iz[me.half] = summed.astype(BF16)
 
-    def first_unit(s, k, masked):
-        b = z - k
+    block_pairs = z // 2 + 1
+
+    def two_blocks(j, part):
+        return jnp.concatenate([kv[z - 2 * j, part], kv[jnp.maximum(z - 2 * j - 1, 0), part]], axis=0)
+
+    def first_unit(s, j, masked):
+        keys, values = two_blocks(j, 0), two_blocks(j, 1)
         for h in range(H):
             cols = pl.ds(h * rows, rows)
-            st = dot_nt(kv[b, 0], qall[s, 0, h]) * scale2
+            st = dot_nt(keys, qall[s, 0, h]) * scale2
             if masked:
-                key_place = lax.broadcasted_iota(jnp.int32, (T, rows), 0) + i * T
-                query_place = lax.broadcasted_iota(jnp.int32, (T, rows), 1) + s * rows
-                st = jnp.where(key_place <= query_place, st, LOW)
-            dp = dot_nt(kv[b, 1], qall[s, 1, h])
-            scores[s, k, :, cols] = st
-            wgrads[s, k, :, cols] = dp
+                row = lax.broadcasted_iota(jnp.int32, (2 * T, rows), 0)
+                near_place = jnp.where(j == 0, i * T, -T)
+                far_place = jnp.where(2 * j + 1 <= z, -2 * T, rows * chips)
+                query_place = lax.broadcasted_iota(jnp.int32, (2 * T, rows), 1) + s * rows
+                st = jnp.where(row + jnp.where(row < T, near_place, far_place) <= query_place, st, LOW)
+            dp = dot_nt(values, qall[s, 1, h])
+            scores[s, j, :, cols] = st
+            wgrads[s, j, :, cols] = dp
             old_top = stat[s, 0:1, cols]
             top = jnp.maximum(old_top, jnp.max(st, axis=0, keepdims=True))
             e = jnp.exp2(st - top)
@@ -268,119 +280,122 @@
         for part in range(2):
             kv_copy(z - t, 1, part).wait_recv()
 
-    def sketch_keys(t):
-        kmt[t] = dot_nt(query_tables, kv[z - t, 0]).astype(BF16)
+    def sketch_keys(j):
+        kmt[j] = dot_nt(query_tables, two_blocks(j, 0)).astype(BF16)
 
     def first_blocks(s, low, high):
-        @pl.when(jnp.logical_and(low == 0, high > 0))
-        def _():
-            first_unit(s, 0, True)
-
-        def over_blocks(k, carry):
-            first_unit(s, k, False)
+        def over_blocks(j, carry):
+            bordering = jnp.logical_or(j == 0, 2 * j == z)
+
+            @pl.when(bordering)
+            def _():
+                first_unit(s, j, True)
+
+            @pl.when(jnp.logical_not(bordering))
+            def _():
+                first_unit(s, j, False)
+
             return carry
 
-        lax.fori_loop(jnp.maximum(low, 1), high, over_blocks, 0)
-
-    def odd_arrivals(t):
-        @pl.when(t + 1 <= z)
+        lax.fori_loop(low, high, over_blocks, 0)
+
+    def even_arrival(t):
+        @pl.when(t <= z)
         def _():
             for part in range(2):
-                kv_copy(z - t - 1, 1, part).wait_recv()
-                relay_kv(z - t - 1, part)
-
+                kv_copy(z - t, 1, part).wait_recv()
+                relay_kv(z - t, part)
+
+    def odd_arrival(t):
         @pl.when(t <= z)
         def _():
             arrived_kv(t)
-            sketch_keys(t)
-
-        @pl.when(t + 1 <= z)
-        def _():
-            sketch_keys(t + 1)
-
-    def first_step(t, carry):
-        @pl.when(lax.rem(t, 2) == 1)
-        def _():
-            odd_arrivals(t)
-
-        @pl.when(t == 0)
-        def _():
-            for part in range(2):
-                wait_piece(0, 1 - c, part)
-
-        if hellos:
-            for n in (1, 2):
-                @pl.when(t == 2 * n)
-                def _():
-                    hear_hello(n - 1)
-                    pass_hello(n)
-
-        @pl.when(t == 2)
-        def _():
-            for n, (step, part) in enumerate(((chips - 1, 0), (1, 1), (chips - 1, 1), (1, 0))):
-                wait_piece(step, c, part)
-                if n < 2:
-                    ring_copies[n].start()
-                sib_copies[(step, part)].start()
-
-        @pl.when(t == 3)
-        def _():
-            for step in (chips - 1, 1):
-                for part in range(2):
-                    wait_piece(step, 1 - c, part)
-
-        @pl.when(t == 4)
-        def _():
-            input_over_y()
-            for part in range(2):
-                wait_piece(2, c, part)
-                sib_copies[(2, part)].start()
-
-        def over_chips(r, carry):
-            active = 3 * ((r + 1) // 2)
-            low = jnp.where(t == active, 0, t)
-            high = jnp.where(t >= active, jnp.minimum(t, z) + 1, 0)
-            first_blocks(rem(x + r * (r + 1) // 2, chips), low, high)
-            return carry
-
-        return lax.fori_loop(0, chips - 1, over_chips, carry)
-
-    lax.fori_loop(0, 6, first_step, 0)
-
-    @pl.when(7 <= z)
-    def _():
-        arrived_kv(7)
-        sketch_keys(7)
-
-    for part in range(2):
-        wait_piece(2, 1 - c, part)
+
+        @pl.when(t // 2 < block_pairs)
+        def _():
+            sketch_keys(t // 2)
+
+    def hand_on(step, part):
+        wait_piece(step, c, part)
+        sib_copies[(step, part)].start()
 
     pairs = chips // 2
 
     def stat_copies(g):
         return [
             remote(
-                stat_send.at[g], stat_recv.at[g, i], st_send_sem.at[g, o - 1], st_recv_sem.at[g, i],
+                stat_send.at[g], stat_recv.at[g, i], pool.at[g * width + o - 1], st_recv_sem.at[g, i],
                 me.at(i=rem(i + o, width)),
             )
             for o in range(1, width)
         ]
 
-    def finish_chips(g, carry):
-        def one_chip(n, carry):
-            s = 2 * g + n
-            first_blocks(s, jnp.where(s == rem(x + 2, chips), 0, 6), z + 1)
-            return carry
-
-        lax.fori_loop(0, 2, one_chip, 0)
-        for n in range(2):
-            stat_send[g, 3 * n:3 * n + 3, :] = stat[2 * g + n, 0:3, :]
-        for copy in stat_copies(g):
-            copy.start()
-        stat_recv[g, i] = stat_send[g]
+    def first_step(n, carry):
+        @pl.when(n == 0)
+        def _():
+            even_arrival(2)
+            for n, (step, part) in enumerate(((chips - 1, 0), (1, 1))):
+                wait_piece(step, c, part)
+                ring_copies[n].start()
+                sib_copies[(step, part)].start()
+            odd_arrival(1)
+            for part in range(2):
+                wait_piece(0, 1 - c, part)
+
+        @pl.when(n == 1)
+        def _():
+            even_arrival(4)
+            hand_on(chips - 1, 1)
+            hand_on(1, 0)
+            if hellos:
+                hear_hello(0)
+                pass_hello(1)
+            odd_arrival(3)
+
+        @pl.when(n == 2)
+        def _():
+            for step in (chips - 1, 1):
+                for part in range(2):
+                    wait_piece(step, 1 - c, part)
+            input_over_y()
+
+        @pl.when(n == 3)
+        def _():
+            hand_on(2, 0)
+            hand_on(2, 1)
+            even_arrival(6)
+            if hellos:
+                hear_hello(1)
+                pass_hello(2)
+
+        @pl.when(n == 4)
+        def _():
+            odd_arrival(5)
+
+        @pl.when(n == 7)
+        def _():
+            odd_arrival(7)
+            for part in range(2):
+                wait_piece(2, 1 - c, part)
+
+        s = jnp.where(n < 2, x, jnp.where(n == 2, x + 1, jnp.where(n == 3, x + chips - 1, x + n - 5)))
+        s = jnp.where(n < 7, rem(s, chips), n - 7)
+        low = jnp.where(n < 2, n, jnp.where(n < 4, 0, jnp.where(n < 7, 2, jnp.where(s == rem(x + 2, chips), 0, 3))))
+        high = jnp.where(n < 2, n + 1, jnp.where(n < 4, 2, jnp.where(n < 7, 3, 4)))
+        first_blocks(s, low, jnp.minimum(high, block_pairs))
+
+        @pl.when(jnp.logical_or(n == 8, n == 10))
+        def _():
+            g = (n - 8) // 2
+            for m in range(2):
+                stat_send[g, 3 * m:3 * m + 3, :] = stat[2 * g + m, 0:3, :]
+            for copy in stat_copies(g):
+                copy.start()
+            stat_recv[g, i] = stat_send[g]
+
         return carry
 
-    lax.fori_loop(0, pairs, finish_chips, 0)
+    lax.fori_loop(0, 11, first_step, 0)
     if hellos:
         hear_hello(2)
     if me.halves > 1:
@@ -390,7 +405,7 @@
         for o in range(1, width):
             p = rem(i + o, width)
             remote(
-                stat_send.at[g], stat_recv.at[g, p], st_send_sem.at[g, 0], st_recv_sem.at[g, p], me.at(i=p)
+                stat_send.at[g], stat_recv.at[g, p], pool.at[0], st_recv_sem.at[g, p], me.at(i=p)
             ).wait_recv()
         for n in range(2):
             first = 3 * n
@@ -406,20 +421,20 @@
             total[2 * g + n, 0:1, :] = top + jnp.log2(weight_sum)
             total[2 * g + n, 1:2, :] = delta_sum / weight_sum
 
-    def second_unit(s, k):
+    def second_unit(s, j):
         lows, grads = [], []
         for h in range(H):
             cols = pl.ds(h * rows, rows)
-            p = jnp.exp2(scores[s, k, :, cols] - total[s, 0:1, cols])
-            g = p * (wgrads[s, k, :, cols] - total[s, 1:2, cols])
+            p = jnp.exp2(scores[s, j, :, cols] - total[s, 0:1, cols])
+            g = p * (wgrads[s, j, :, cols] - total[s, 1:2, cols])
             lows.append(p.astype(BF16))
             g = g.astype(BF16)
             grads.append(g)
-            dq_acc[s] += dot_nn(kmt[k, h * SK:(h + 1) * SK, :], g)
+            dq_acc[s] += dot_nn(kmt[j, h * SK:(h + 1) * SK, :], g)
         low = jnp.concatenate(lows, axis=1)
         grad = jnp.concatenate(grads, axis=1)
-        dkv_acc[k, 0] += dot_nn(grad, qall[s, 0].reshape(H * rows, F))
-        dkv_acc[k, 1] += dot_nn(low, qall[s, 1].reshape(H * rows, F))
+        dkv_acc[j, 0] += dot_nn(grad, qall[s, 0].reshape(H * rows, F))
+        dkv_acc[j, 1] += dot_nn(low, qall[s, 1].reshape(H * rows, F))
 
     def dkv_copy(k, b):
         return remote(dkv_send.at[k], dkv_recv.at[z], dkv_send_sem.at[k], dkv_recv_sem.at[z], me.at(z=b))
@@ -438,42 +453,85 @@
     def dq_copy(p):
         return remote(dq_send.at[p], dq_recv.at[i], dq_send_sem.at[p], dq_recv_sem.at[i], me.at(i=p))
 
-    near_blocks = (z + 2) // 2
-    add_statistics(0)
-
-    def half_blocks(k, carry):
+    near_pairs = (block_pairs + 1) // 2
+    def second_step(m, carry):
+        n = m - near_pairs
+        j = jnp.where(n < 0, m, block_pairs - 1 - n)
+
+        @pl.when(m == 0)
+        def _():
+            add_statistics(0)
+
+        @pl.when(n == 0)
+        def _():
+            add_statistics(1)
+
+        @pl.when(n == block_pairs - near_pairs)
+        def _():
+            send_dq(0)
+
         def over_chips(s, carry):
-            second_unit(s, k)
+            second_unit(s, j)
             return carry
 
-        return lax.fori_loop(0, 2, over_chips, carry)
-
-    lax.fori_loop(0, near_blocks, half_blocks, 0)
-    add_statistics(1)
-
-    def second_step(n, carry):
-        k = z - n
-
-        @pl.when(k == near_blocks - 1)
-        def _():
-            send_dq(0)
-
-        def over_chips(s, carry):
-            second_unit(s, k)
-            return carry
-
-        lax.fori_loop(jnp.where(k < near_blocks, 2, 0), chips, over_chips, 0)
-        dkv_send[k, 0:SK, :] = dot_nt(key_table, (dkv_acc[k, 0] * scale).astype(BF16)).astype(BF16)
-        dkv_send[k, SK:, :] = dot_nt(value_table, dkv_acc[k, 1].astype(BF16)).astype(BF16)
-
-        @pl.when(k > 0)
-        def _():
-            dkv_copy(k, n).start()
+        first = jnp.where(n < 0, 0, jnp.where(j < near_pairs, 2, 0))
+        lax.fori_loop(first, jnp.where(n < 0, 2, chips), over_chips, 0)
+
+        @pl.when(n >= 0)
+        def _():
+            key_part = dot_nt(key_table, (dkv_acc[j, 0] * scale).astype(BF16)).astype(BF16)
+            value_part = dot_nt(value_table, dkv_acc[j, 1].astype(BF16)).astype(BF16)
+            for b in range(2):
+                dkv_send[2 * j + b, 0:SK, :] = key_part[:, b * T:(b + 1) * T]
+                dkv_send[2 * j + b, SK:, :] = value_part[:, b * T:(b + 1) * T]
+
+        @pl.when(jnp.logical_and(n >= 0, 2 * j + 1 <= z))
+        def _():
+            dkv_copy(2 * j + 1, z - 2 * j - 1).start()
+
+        @pl.when(jnp.logical_and(n >= 0, j > 0))
+        def _():
+            dkv_copy(2 * j, z - 2 * j).start()
 
         return carry
 
-    lax.fori_loop(0, z + 1, second_step, 0)
+    lax.fori_loop(0, near_pairs + block_pairs, second_step, 0)
     send_dq(1)
+
+    for copy in own_copies + ring_copies + list(sib_copies.values()) + iy_copies:
+        copy.wait_send()
+    if me.halves > 1:
+        iz_copy.wait_send()
+
+    for g in range(pairs):
+        for copy in stat_copies(g):
+            copy.wait_send()
+    for p in range(width):
+        @pl.when(p != i)
+        def _():
+            dq_copy(p).wait_send()
+
+    def left_kv(n, carry):
+        b = z - 2 * n
+
+        for part in range(2):
+            @pl.when(z + 2 < planes)
+            def _():
+                kv_copy(b, 2, part).wait_send()
+
+            @pl.when(z + 1 < planes)
+            def _():
+                kv_copy(b, 1, part).wait_send()
+
+        return carry
+
+    lax.fori_loop(0, z // 2 + 1, left_kv, 0)
+
+    def left_dkv(k, carry):
+        dkv_copy(k, z - k).wait_send()
+        return carry
+
+    lax.fori_loop(1, z + 1, left_dkv, 0)
 
     if me.halves > 1:
         away = 1 - me.half
@@ -510,14 +568,18 @@
     grads_high = grads.astype(BF16)
     grads_low = (grads - grads_high.astype(F32)).astype(BF16)
     product = dot_nt(masked_high, grads_high) + (dot_nt(masked_high, grads_low) + dot_nt(masked_low, grads_high))
-    products[...] = product.reshape(DOCS_MOST, SK, 4 * SK).astype(BF16)
+    product = product.reshape(DOCS_MOST // 2, 2, SK, 4 * SK)
+    products[:, 0:2] = product[:, :, :, 0:2 * SK].astype(BF16)
+    value_product = product[:, :, :, 2 * SK:]
+    moved = pltpu.roll(value_product[:, 1].reshape(DOCS_MOST // 2 * SK, 2 * SK), SK, 1)
+    products[:, 2] = (value_product[:, 0] + moved.reshape(DOCS_MOST // 2, SK, 2 * SK)).astype(BF16)
 
     def part(p, y):
-        return products.at[pl.ds(p * 2, 2), pl.ds(pl.multiple_of(y * band, band), band), :]
+        return products.at[p, :, pl.ds(pl.multiple_of(y * band, band), band), :]
 
     my_slot = place_in_group * ys + me.y
     near_copies = [
-        remote(part(p, y), near.at[my_slot], near_send_sem.at[n], near_recv_sem.at[my_slot], me.at(i=group_first + p, y=y))
+        remote(part(p, y), near.at[my_slot], pool.at[n], near_recv_sem.at[my_slot], me.at(i=group_first + p, y=y))
         for n, (p, y) in enumerate(near_peers)
     ]
     for copy in near_copies:
@@ -525,48 +587,61 @@
     summed = part(place_in_group, me.y)[...].astype(F32)
     for p, y in near_peers:
         slot = p * ys + y
-        remote(near.at[slot], near.at[slot], near_send_sem.at[0], near_recv_sem.at[slot], me.at(i=group_first + p, y=y)).wait_recv()
+        remote(near.at[slot], near.at[slot], pool.at[0], near_recv_sem.at[slot], me.at(i=group_first + p, y=y)).wait_recv()
         summed = summed + near[slot].astype(F32)
     plane_docs[i] = summed.astype(BF16)
 
     plane_copies = [
-        remote(plane_docs.at[i], plane_docs.at[i], plane_send_sem.at[o - 1], plane_recv_sem.at[i], me.at(i=rem(i + o, width)))
+        remote(plane_docs.at[i], plane_docs.at[i], dq_send_sem.at[o - 1], plane_recv_sem.at[i], me.at(i=rem(i + o, width)))
         for o in range(1, width)
     ]
     for copy in plane_copies:
         copy.start()
     for o in range(1, width):
         p = rem(i + o, width)
-        remote(plane_docs.at[p], plane_docs.at[p], plane_send_sem.at[0], plane_recv_sem.at[p], me.at(i=p)).wait_recv()
-
-    def gather_row(fz, carry):
+        remote(plane_docs.at[p], plane_docs.at[p], dq_send_sem.at[0], plane_recv_sem.at[p], me.at(i=p)).wait_recv()
+
+    for copy in near_copies:
+        copy.wait_send()
+
+    my_line = z * halves + me.half
+    own = band // halves
+
+    def far_copy(fz, half):
+        slot = fz * halves + half
+        return remote(far_send.at[slot], far.at[my_line], pool.at[slot], far_recv_sem.at[my_line], me.at(z=fz, half=half))
+
+    def gather_row(n, carry):
+        fz = rem(z + n, planes)
         row = fz * width + i
-        found = jnp.zeros((band, 4 * SK), F32)
+        found = jnp.zeros((band, 2 * SK), F32)
+        values = [jnp.zeros((band, 2 * SK), F32)] * 2
         for j in range(width):
             for e in range(2):
-                chosen = jnp.broadcast_to(slot_row[:, 2 * j + e:2 * j + e + 1], (band, 4 * SK)) == row
+                chosen = jnp.broadcast_to(slot_row[:, 2 * j + e:2 * j + e + 1], (band, 2 * SK)) == row
                 found = found + jnp.where(chosen, plane_docs[j, e].astype(F32), 0.0)
-        own = band // halves
+                values[e] = values[e] + jnp.where(chosen, plane_docs[j, 2].astype(F32), 0.0)
+        lanes = lax.broadcasted_iota(jnp.int32, (band, 2 * SK), 1)
+        value_rows = jnp.where(lanes < SK, values[0] + pltpu.roll(values[1], SK, 1), 0.0)
         for half in range(halves):
-            rows_half = found[half * own:(half + 1) * own, :]
-            both = jnp.concatenate([rows_half[:, 0:2 * SK], rows_half[:, 2 * SK:]], axis=0)
+            mine_of = slice(half * own, (half + 1) * own)
+            both = jnp.concatenate([found[mine_of], value_rows[mine_of]], axis=0)
             far_send[fz * halves + half] = both.astype(BF16)
+
+            @pl.when(jnp.logical_or(fz != z, me.half != half))
+            def _():
+                far_copy(fz, half).start()
+
         return carry
 
     lax.fori_loop(0, planes, gather_row, 0)
-    my_line = z * halves + me.half
-    far_copies = [
-        remote(far_send.at[fz * halves + half], far.at[my_line], far_send_sem.at[n], far_recv_sem.at[my_line], me.at(z=fz, half=half))
-        for n, (fz, half) in enumerate(far_peers)
-    ]
-    for copy in far_copies:
-        copy.start()
+    for copy in plane_copies:
+        copy.wait_send()
     result = far_send[my_line].astype(F32)
     for fz, half in far_peers:
         slot = fz * halves + half
-        remote(far.at[slot], far.at[slot], far_send_sem.at[0], far_recv_sem.at[slot], me.at(z=fz, half=half)).wait_recv()
+        remote(far.at[slot], far.at[slot], pool.at[0], far_recv_sem.at[slot], me.at(z=fz, half=half)).wait_recv()
         result = result + far[slot].astype(F32)
-    own = band // halves
     query_key, value_only = result[0:own], result[own:]
     key_query, moved_value = pltpu.roll(query_key, SK, 1), pltpu.roll(value_only, SK, 1)
     first_half = lax.broadcasted_iota(jnp.int32, (1, 2 * SK), 1) < SK
@@ -575,41 +650,8 @@
             out_ref[0, p:p + 1, pair * 2 * SK:(pair + 1) * 2 * SK] = jnp.where(
                 first_half, even[2 * pair:2 * pair + 1], odd[2 * pair + 1:2 * pair + 2]
             )
-
-    for copy in own_copies + ring_copies + list(sib_copies.values()) + iy_copies + near_copies + plane_copies + far_copies:
-        copy.wait_send()
-    if me.halves > 1:
-        iz_copy.wait_send()
-
-    for g in range(pairs):
-        for copy in stat_copies(g):
-            copy.wait_send()
-    for p in range(width):
-        @pl.when(p != i)
-        def _():
-            dq_copy(p).wait_send()
-
-    def left_kv(n, carry):
-        b = z - 2 * n
-
-        for part in range(2):
-            @pl.when(z + 2 < planes)
-            def _():
-                kv_copy(b, 2, part).wait_send()
-
-            @pl.when(z + 1 < planes)
-            def _():
-                kv_copy(b, 1, part).wait_send()
-
-        return carry
-
-    lax.fori_loop(0, z // 2 + 1, left_kv, 0)
-
-    def left_dkv(k, carry):
-        dkv_copy(k, z - k).wait_send()
-        return carry
-
-    lax.fori_loop(1, z + 1, left_dkv, 0)
+    for fz, half in far_peers:
+        far_copy(fz, half).wait_send()
 
 
 def sketches_of(
@@ -628,21 +670,20 @@
     return pl.pallas_call(
         kernel,
         out_shape=jax.ShapeDtypeStruct((1, 3, band // halves * SK), F32),
-        in_specs=[pl.BlockSpec(memory_space=pltpu.SMEM)] * 2 + [pl.BlockSpec(memory_space=pl.ANY)] * 5
-        + [pl.BlockSpec(memory_space=pltpu.VMEM)] * 4,
+        in_specs=[pl.BlockSpec(memory_space=pl.ANY)] * 11,
         out_specs=pl.BlockSpec(memory_space=pltpu.VMEM),
         scratch_shapes=[
             vmem((chips, 2, H, rows, F), BF16),
             vmem((planes, 2, T, F), BF16),
-            vmem((chips, planes, T, H * rows), F32),
-            vmem((chips, planes, T, H * rows), F32),
+            vmem((chips, planes // 2, 2 * T, H * rows), F32),
+            vmem((chips, planes // 2, 2 * T, H * rows), F32),
             vmem((chips, 8, H * rows), F32),
-            vmem((planes, H * SK, T), BF16),
+            vmem((planes // 2, H * SK, 2 * T), BF16),
             vmem((pairs, 8, H * rows), F32),
             vmem((pairs, width, 8, H * rows), F32),
             vmem((chips, 8, H * rows), F32),
             vmem((chips, SK, rows), F32),
-            vmem((planes, 2, T, F), F32),
+            vmem((planes // 2, 2, 2 * T, F), F32),
             vmem((planes, 2 * SK, T), BF16),
             vmem((planes, 2 * SK, T), BF16),
             vmem((width, SK, T), BF16),
@@ -650,22 +691,23 @@
             vmem((ys, SK, T), BF16),
             vmem((halves, SK, T), BF16),
             vmem((4 * SK, T), F32),
-            vmem((DOCS_MOST, SK, 4 * SK), BF16),
-            vmem((GROUP * ys, 2, band, 4 * SK), BF16),
-            vmem((width, 2, band, 4 * SK), BF16),
+            vmem((DOCS_MOST // 2, 3, SK, 2 * SK), BF16),
+            vmem((GROUP * ys, 3, band, 2 * SK), BF16),
+            vmem((width, 3, band, 2 * SK), BF16),
             vmem((line, 2 * band // halves, 2 * SK), BF16),
             vmem((line, 2 * band // halves, 2 * SK), BF16),
             vmem(layer_input.shape, BF16),
-            dma((2 + 2 * H + 1,)), pltpu.SemaphoreType.REGULAR((3,)),
+            pltpu.SMEM(doc_starts.shape, jnp.int32), pltpu.SMEM(doc_rows.shape, jnp.int32),
+            vmem(input_hash.shape, jnp.int32), vmem(query_hash.shape, jnp.int32),
+            vmem(key_hash.shape, jnp.int32), vmem(value_hash.shape, jnp.int32),
+            dma((2 + 2 * H + 7,)), pltpu.SemaphoreType.REGULAR((3,)),
             dma((chips, 2, 2)), dma((3, 2)), dma((2,)), dma((3, 2)),
-            dma((planes, 2, 2)), dma((planes, 2)),
-            dma((pairs, width)), dma((pairs, width)),
+            dma(((planes + 1) // 2, 2, 2)), dma((planes, 2)),
+            dma((max(pairs * width, GROUP * ys, line),)), dma((pairs, width)),
             dma((planes,)), dma((planes,)),
             dma((width,)), dma((width,)),
             dma((ys,)), dma((ys,)), dma((halves,)), dma((halves,)),
-            dma((GROUP * ys,)), dma((GROUP * ys,)),
-            dma((width,)), dma((width,)),
-            dma((line,)), dma((line,)),
+            dma((GROUP * ys,)), dma((width,)), dma((line,)),
         ],
         compiler_params=pltpu.CompilerParams(
             collective_id=0, has_side_effects=True, vmem_limit_bytes=56 * 1024 * 1024

time: 80 us -> 76.4 us (0.955)
  Pallas kernels: 78.4 us -> 74.9 us
    pallas_call x1, Pallas kernels: 78.4 us -> 74.9 us  [sketches_of(): pl.pallas_call(kernel, out_shape=jax.ShapeDtypeStruct((1, 3, band // halv...]
where the time goes in v4:
time: 76.4 us; the launch traced here: 76.2 us
  Pallas kernels  74.9 us (98%)
  local copies, waits for them, and re-layouts  1.3 us (2%)
    pallas_call x1, Pallas kernels, sketches_of(): pl.pallas_call(kernel, out_shape=jax.ShapeDtypeStruct((1, 3, band // halv...  74.9 us

profile of v4, /device:TPU:1, one launch (start us, length us, event | category | flops | bytes accessed | tf_op | source)
XLA Modules:
  0.0 76.2 jit_solution(14155743432031957310)
XLA Ops:
  0.0 74.9 %sketches.1 = f32[1,3,512]{2,1,0:T(4,128)} custom-call(s32[64]{0:T(128)} %starts_ref.1, s32[64]{0:T(128)} %targets_ref.1, bf16[128,1024]{1,0:T(8,128)(2,1)} %x_ref.1, bf16[128,512]{1,0:T(8,128)(2,1)} %q_ref.1, bf16[128,128]{1,0:T(8,128)(2,1)} %k_ref.1, bf16[128,128]{1,0:T(8,128)(2,1)} %v_ref.1, bf16[128,512]{1,0:T(8,128)(2,1)} %do_ref.1, s32[2,1024]{1,0:T(2,128)} %xh_ref.1, ...), custom_call_target="tpu_custom_call" | custom-call | tf_op jit(solution)/shard_map/sketches/pallas_call | solution.py:670
  74.9 1.3 %copy.12 = f32[1,3,512]{2,0,1:T(1,128)} copy(f32[1,3,512]{2,1,0:T(4,128)} %sketches.1) | data formatting | bytes 12288 | tf_op jit(solution)/shard_map/sketches/pallas_call | solution.py:670

commit v5 on v4

--- a/solution.py
+++ b/solution.py
@@ -39,6 +39,10 @@
 
 def rem(value, count):
     return lax.rem(value + count, count)
+
+
+def far_first(count):
+    return sorted(range(1, count), key=lambda o: -min(o, count - o))
 
 
 class Place:
@@ -81,7 +85,7 @@
     out_ref,
     qall, kv, scores, wgrads, stat, kmt, stat_send, stat_recv, total, dq_acc, dkv_acc,
     dkv_send, dkv_recv, dq_send, dq_recv, iy, iz, grad_sum,
-    products, near, plane_docs, far_send, far,
+    products, near, plane_docs, doc_target, far_send, far,
     inputs, starts, targets, input_hash, query_hash, key_hash, value_hash, input_sem, hello, q_recv, q_own, q_ring, q_sib, kv_send_sem, kv_recv_sem, pool, st_recv_sem,
     dkv_send_sem, dkv_recv_sem, dq_send_sem, dq_recv_sem, iy_send_sem, iy_recv_sem, iz_send_sem, iz_recv_sem,
     near_recv_sem, plane_recv_sem, far_recv_sem,
@@ -97,8 +101,10 @@
     place_in_group = lax.rem(i, GROUP)
     group_first = i - place_in_group
     near_peers = []
-    for o in range(1, GROUP * ys):
-        near_peers.append((rem(place_in_group + o // ys, GROUP), rem(me.y + o % ys, ys)))
+    for p in far_first(GROUP) + [0]:
+        for y in far_first(ys) + [0]:
+            if (p, y) != (0, 0):
+                near_peers.append((rem(place_in_group + p, GROUP), rem(me.y + y, ys)))
     far_peers = []
     for o in range(1, planes * halves):
         far_peers.append((rem(z + o // halves, planes), rem(me.half + o % halves, halves)))
@@ -119,7 +125,7 @@
         pl.semaphore_wait(hello.at[n], 2)
 
     friends += [me.at(y=rem(me.y + o, ys)) for o in range(1, ys)]
-    friends += [me.at(i=rem(i + o, width)) for o in range(1, width)]
+    friends += [me.at(i=rem(i + o, width)) for o in far_first(width)]
     greet(friends)
 
     mine = pl.ds(pl.multiple_of(c * T, T), T)
@@ -231,6 +237,8 @@
     slot_row = jnp.full((1, T), -1, jnp.int32)
     for d in range(doc_count):
         slot_row = jnp.where(slot_doc == d, targets[d], slot_row)
+    for n in range(2 * width):
+        doc_target[n] = jnp.broadcast_to(slot_row[:, n:n + 1], doc_target.shape[1:])
 
     iy_copies = [
         remote(iy.at[me.y], iy.at[me.y], iy_send_sem.at[o - 1], iy_recv_sem.at[me.y], me.at(y=rem(me.y + o, me.ys)))
@@ -327,7 +335,7 @@
                 stat_send.at[g], stat_recv.at[g, i], pool.at[g * width + o - 1], st_recv_sem.at[g, i],
                 me.at(i=rem(i + o, width)),
             )
-            for o in range(1, width)
+            for o in far_first(width)
         ]
 
     def first_step(n, carry):
@@ -402,7 +410,7 @@
         iz_copy.start()
 
     def add_statistics(g):
-        for o in range(1, width):
+        for o in far_first(width):
             p = rem(i + o, width)
             remote(
                 stat_send.at[g], stat_recv.at[g, p], pool.at[0], st_recv_sem.at[g, p], me.at(i=p)
@@ -552,7 +560,7 @@
 
     dq_recv[i] = dq_send[i]
     lax.fori_loop(z + 1, planes, add_kv, 0)
-    for o in range(1, width):
+    for o in far_first(width):
         p = rem(i + o, width)
         remote(dq_send.at[p], dq_recv.at[p], dq_send_sem.at[0], dq_recv_sem.at[p], me.at(i=p)).wait_recv()
     query_sum = dq_recv[0].astype(F32)
@@ -593,11 +601,11 @@
 
     plane_copies = [
         remote(plane_docs.at[i], plane_docs.at[i], dq_send_sem.at[o - 1], plane_recv_sem.at[i], me.at(i=rem(i + o, width)))
-        for o in range(1, width)
+        for o in far_first(width)
     ]
     for copy in plane_copies:
         copy.start()
-    for o in range(1, width):
+    for o in far_first(width):
         p = rem(i + o, width)
         remote(plane_docs.at[p], plane_docs.at[p], dq_send_sem.at[0], plane_recv_sem.at[p], me.at(i=p)).wait_recv()
 
@@ -618,7 +626,7 @@
         values = [jnp.zeros((band, 2 * SK), F32)] * 2
         for j in range(width):
             for e in range(2):
-                chosen = jnp.broadcast_to(slot_row[:, 2 * j + e:2 * j + e + 1], (band, 2 * SK)) == row
+                chosen = doc_target[2 * j + e] == row
                 found = found + jnp.where(chosen, plane_docs[j, e].astype(F32), 0.0)
                 values[e] = values[e] + jnp.where(chosen, plane_docs[j, 2].astype(F32), 0.0)
         lanes = lax.broadcasted_iota(jnp.int32, (band, 2 * SK), 1)
@@ -694,6 +702,7 @@
             vmem((DOCS_MOST // 2, 3, SK, 2 * SK), BF16),
             vmem((GROUP * ys, 3, band, 2 * SK), BF16),
             vmem((width, 3, band, 2 * SK), BF16),
+            vmem((2 * width, band, 2 * SK), jnp.int32),
             vmem((line, 2 * band // halves, 2 * SK), BF16),
             vmem((line, 2 * band // halves, 2 * SK), BF16),
             vmem(layer_input.shape, BF16),

time: 76.4 us -> 76 us (level)
  no operation moved by 1% of the time
where the time goes in v5:
time: 76 us; the launch traced here: 75.9 us
  Pallas kernels  74.6 us (98%)
  local copies, waits for them, and re-layouts  1.3 us (2%)
    pallas_call x1, Pallas kernels, sketches_of(): pl.pallas_call(kernel, out_shape=jax.ShapeDtypeStruct((1, 3, band // halv...  74.6 us

profile of v5, /device:TPU:1, one launch (start us, length us, event | category | flops | bytes accessed | tf_op | source)
XLA Modules:
  0.0 75.9 jit_solution(4152103897194332662)
XLA Ops:
  0.0 74.6 %sketches.1 = f32[1,3,512]{2,1,0:T(4,128)} custom-call(s32[64]{0:T(128)} %starts_ref.1, s32[64]{0:T(128)} %targets_ref.1, bf16[128,1024]{1,0:T(8,128)(2,1)} %x_ref.1, bf16[128,512]{1,0:T(8,128)(2,1)} %q_ref.1, bf16[128,128]{1,0:T(8,128)(2,1)} %k_ref.1, bf16[128,128]{1,0:T(8,128)(2,1)} %v_ref.1, bf16[128,512]{1,0:T(8,128)(2,1)} %do_ref.1, s32[2,1024]{1,0:T(2,128)} %xh_ref.1, ...), custom_call_target="tpu_custom_call" | custom-call | tf_op jit(solution)/shard_map/sketches/pallas_call | solution.py:678
  74.6 1.3 %copy.12 = f32[1,3,512]{2,0,1:T(1,128)} copy(f32[1,3,512]{2,1,0:T(4,128)} %sketches.1) | data formatting | bytes 12288 | tf_op jit(solution)/shard_map/sketches/pallas_call | solution.py:678

commit v6 on v5

--- a/solution.py
+++ b/solution.py
@@ -84,10 +84,10 @@
     starts_ref, targets_ref, x_ref, q_ref, k_ref, v_ref, do_ref, xh_ref, qh_ref, kh_ref, vh_ref,
     out_ref,
     qall, kv, scores, wgrads, stat, kmt, stat_send, stat_recv, total, dq_acc, dkv_acc,
-    dkv_send, dkv_recv, dq_send, dq_recv, iy, iz, grad_sum,
+    dkv_send, dkv_recv, dkv_up, dq_send, dq_recv, iy, iz, grad_sum,
     products, near, plane_docs, doc_target, far_send, far,
     inputs, starts, targets, input_hash, query_hash, key_hash, value_hash, input_sem, hello, q_recv, q_own, q_ring, q_sib, kv_send_sem, kv_recv_sem, pool, st_recv_sem,
-    dkv_send_sem, dkv_recv_sem, dq_send_sem, dq_recv_sem, iy_send_sem, iy_recv_sem, iz_send_sem, iz_recv_sem,
+    dkv_send_sem, dkv_recv_sem, up_recv_sem, dq_send_sem, dq_recv_sem, iy_send_sem, iy_recv_sem, iz_send_sem, iz_recv_sem,
     near_recv_sem, plane_recv_sem, far_recv_sem,
 ):
     me = Place()
@@ -444,8 +444,32 @@
         dkv_acc[j, 0] += dot_nn(grad, qall[s, 0].reshape(H * rows, F))
         dkv_acc[j, 1] += dot_nn(low, qall[s, 1].reshape(H * rows, F))
 
+    odd_plane = lax.rem(z, 2) == 1
+    even_plane = lax.rem(z, 2) == 0
+
+    def hand_down(k):
+        return remote(
+            dkv_send.at[k], dkv_up.at[z - k], dkv_send_sem.at[k], up_recv_sem.at[z - k], me.at(z=rem(z - 1, planes))
+        )
+
     def dkv_copy(k, b):
-        return remote(dkv_send.at[k], dkv_recv.at[z], dkv_send_sem.at[k], dkv_recv_sem.at[z], me.at(z=b))
+        return remote(
+            dkv_send.at[k], dkv_recv.at[z // 2], dkv_send_sem.at[k], dkv_recv_sem.at[z // 2], me.at(z=b)
+        )
+
+    def add_and_send(j):
+        for k in (2 * j + 1, 2 * j):
+            @pl.when(k <= z)
+            def _():
+                b = z - k
+                remote(
+                    dkv_send.at[0], dkv_up.at[b], dkv_send_sem.at[0], up_recv_sem.at[b], me.at(z=rem(z + 1, planes))
+                ).wait_recv()
+                dkv_send[k] = (dkv_send[k].astype(F32) + dkv_up[b].astype(F32)).astype(BF16)
+
+                @pl.when(k > 0)
+                def _():
+                    dkv_copy(k, b).start()
 
     def send_dq(g):
         for s in (2 * g, 2 * g + 1):
@@ -493,18 +517,26 @@
                 dkv_send[2 * j + b, 0:SK, :] = key_part[:, b * T:(b + 1) * T]
                 dkv_send[2 * j + b, SK:, :] = value_part[:, b * T:(b + 1) * T]
 
-        @pl.when(jnp.logical_and(n >= 0, 2 * j + 1 <= z))
-        def _():
-            dkv_copy(2 * j + 1, z - 2 * j - 1).start()
-
-        @pl.when(jnp.logical_and(n >= 0, j > 0))
-        def _():
-            dkv_copy(2 * j, z - 2 * j).start()
+        @pl.when(jnp.logical_and(n >= 0, odd_plane))
+        def _():
+            hand_down(2 * j + 1).start()
+
+        @pl.when(jnp.logical_and(n >= 0, jnp.logical_and(odd_plane, j > 0)))
+        def _():
+            hand_down(2 * j).start()
+
+        @pl.when(jnp.logical_and(n >= 1, even_plane))
+        def _():
+            add_and_send(j + 1)
 
         return carry
 
     lax.fori_loop(0, near_pairs + block_pairs, second_step, 0)
     send_dq(1)
+
+    @pl.when(even_plane)
+    def _():
+        add_and_send(0)
 
     for copy in own_copies + ring_copies + list(sib_copies.values()) + iy_copies:
         copy.wait_send()
@@ -553,13 +585,15 @@
     kv_factor = math.sqrt(SK / (F * heads))
     grad_sum[SK:3 * SK, :] = dkv_send[0].astype(F32) * kv_factor
 
-    def add_kv(b, carry):
-        remote(dkv_send.at[0], dkv_recv.at[b], dkv_send_sem.at[0], dkv_recv_sem.at[b], me.at(z=rem(z + 1, planes))).wait_recv()
-        grad_sum[SK:3 * SK, :] += dkv_recv[b].astype(F32) * kv_factor
+    def add_kv(m, carry):
+        remote(
+            dkv_send.at[0], dkv_recv.at[m], dkv_send_sem.at[0], dkv_recv_sem.at[m], me.at(z=rem(z + 1, planes))
+        ).wait_recv()
+        grad_sum[SK:3 * SK, :] += dkv_recv[m].astype(F32) * kv_factor
         return carry
 
     dq_recv[i] = dq_send[i]
-    lax.fori_loop(z + 1, planes, add_kv, 0)
+    lax.fori_loop(z // 2 + 1, planes // 2, add_kv, 0)
     for o in far_first(width):
         p = rem(i + o, width)
         remote(dq_send.at[p], dq_recv.at[p], dq_send_sem.at[0], dq_recv_sem.at[p], me.at(i=p)).wait_recv()
@@ -693,6 +727,7 @@
             vmem((chips, SK, rows), F32),
             vmem((planes // 2, 2, 2 * T, F), F32),
             vmem((planes, 2 * SK, T), BF16),
+            vmem((planes // 2, 2 * SK, T), BF16),
             vmem((planes, 2 * SK, T), BF16),
             vmem((width, SK, T), BF16),
             vmem((width, SK, T), BF16),
@@ -713,7 +748,7 @@
             dma((chips, 2, 2)), dma((3, 2)), dma((2,)), dma((3, 2)),
             dma(((planes + 1) // 2, 2, 2)), dma((planes, 2)),
             dma((max(pairs * width, GROUP * ys, line),)), dma((pairs, width)),
-            dma((planes,)), dma((planes,)),
+            dma((planes,)), dma((planes // 2,)), dma((planes,)),
             dma((width,)), dma((width,)),
             dma((ys,)), dma((ys,)), dma((halves,)), dma((halves,)),
             dma((GROUP * ys,)), dma((width,)), dma((line,)),

time: 76 us -> 76.2 us (level)
  no operation moved by 1% of the time
where the time goes in v6:
time: 76.2 us; the launch traced here: 76 us
  Pallas kernels  74.7 us (98%)
  local copies, waits for them, and re-layouts  1.3 us (2%)
    pallas_call x1, Pallas kernels, sketches_of(): pl.pallas_call(kernel, out_shape=jax.ShapeDtypeStruct((1, 3, band // halv...  74.7 us

profile of v6, /device:TPU:1, one launch (start us, length us, event | category | flops | bytes accessed | tf_op | source)
XLA Modules:
  0.0 76.0 jit_solution(3068653589825927445)
XLA Ops:
  0.0 74.7 %sketches.1 = f32[1,3,512]{2,1,0:T(4,128)} custom-call(s32[64]{0:T(128)} %starts_ref.1, s32[64]{0:T(128)} %targets_ref.1, bf16[128,1024]{1,0:T(8,128)(2,1)} %x_ref.1, bf16[128,512]{1,0:T(8,128)(2,1)} %q_ref.1, bf16[128,128]{1,0:T(8,128)(2,1)} %k_ref.1, bf16[128,128]{1,0:T(8,128)(2,1)} %v_ref.1, bf16[128,512]{1,0:T(8,128)(2,1)} %do_ref.1, s32[2,1024]{1,0:T(2,128)} %xh_ref.1, ...), custom_call_target="tpu_custom_call" | custom-call | tf_op jit(solution)/shard_map/sketches/pallas_call | solution.py:712
  74.7 1.3 %copy.12 = f32[1,3,512]{2,0,1:T(1,128)} copy(f32[1,3,512]{2,1,0:T(4,128)} %sketches.1) | data formatting | bytes 12288 | tf_op jit(solution)/shard_map/sketches/pallas_call | solution.py:712
